TPU v7x, 256 devices: a whole 4x4x8 slice. The times are simulated.
256 devices in a mesh: blk: 32 (over z, x_hi, core), tensor: 8 (over y, x_lo).
Axes of the slice: x: 4 (x_hi: 2, x_lo: 2; x = x_hi * 2 + x_lo), y: 4, z: 8, core: 2. Of those that a mesh axis runs over, the one named last changes fastest.
Arguments:
- inputs: bfloat16 [10240, 8192], P('blk'), may hold values from -96 to 96, as said below
- query_weight: bfloat16 [8192, 4096], P('blk', 'tensor'), may hold values from -0.0625 to 0.0625
- kv_weight: bfloat16 [2, 8192, 512], P(None, 'blk'), may hold values from -0.0625 to 0.0625
- out_grad: bfloat16 [10240, 4096], P('blk', 'tensor'), may hold values from -6 to 6
Outputs:
- attention: bfloat16 [10240, 4096], P('blk', 'tensor')
- grad_query_weight: bfloat16 [8192, 4096], P('blk', 'tensor')
- grad_kv_weight: bfloat16 [2, 8192, 512], P(None, 'blk')
- grad_inputs: bfloat16 [10240, 8192], P(('blk', 'tensor'))
Inputs may be any that keep to these rules, and one draw needn't show every extreme that they name: `inputs`: real entries.
All inputs are finite; a program needn't handle non-finite values.
Results may differ from a plain program's by a relative error of at most 0.022.
Values may be sent and summed in bfloat16 or wider, within the bound.
A program may use at most 128 MiB of HBM per device.

v0:
```python
import math

import jax
import jax.numpy as jnp
from jax import lax
from jax.sharding import PartitionSpec as P

HD = 128
QH = 32
KVH = 4
L = 320


def rotary(states, direction):
    length = states.shape[1]
    head_width = states.shape[3]
    half_width = head_width // 2
    freq_index = jnp.arange(half_width, dtype=jnp.float32)
    frequency = jnp.exp(freq_index * (-2.0 * math.log(10000.0) / head_width))
    positions = jnp.arange(length, dtype=jnp.float32)
    angles = positions[:, None] * frequency[None, :]
    cosine = jnp.cos(angles)[None, :, None, :]
    sine_part = direction * jnp.sin(angles)[None, :, None, :]
    first_half = states[..., :half_width]
    second_half = states[..., half_width:]
    return jnp.concatenate(
        [
            first_half * cosine - second_half * sine_part,
            second_half * cosine + first_half * sine_part,
        ],
        axis=-1,
    )


def attend(query_states, key_states, value_states, grad_out, head_block):
    highest = lax.Precision.HIGHEST
    length = query_states.shape[1]
    score_scale = 1.0 / math.sqrt(query_states.shape[4])
    scores = (
        jnp.einsum("slkgd,smkd->skglm", query_states, key_states, precision=highest) * score_scale
    )
    row_pos = jnp.arange(length)[:, None]
    col_pos = jnp.arange(length)[None, :]
    allowed = col_pos <= row_pos
    scores = jnp.where(allowed, scores, -1e30)
    row_max = jnp.max(scores, axis=-1, keepdims=True)
    expd = jnp.exp(scores - row_max)
    row_total = jnp.sum(expd, axis=-1, keepdims=True)
    probabilities = expd / row_total
    outputs = jnp.einsum("skglm,smkd->slkgd", probabilities, value_states, precision=highest)
    grad_probs = jnp.einsum("slkgd,smkd->skglm", grad_out, value_states, precision=highest)
    row_delta = jnp.einsum("slkgd,slkgd->skgl", grad_out, outputs, precision=highest)
    grad_scores = probabilities * (grad_probs - row_delta[..., None])
    grad_queries = (
        jnp.einsum("skglm,smkd->slkgd", grad_scores, key_states, precision=highest) * score_scale
    )
    key_heads = (
        jnp.einsum("skglm,slkgd->smkgd", grad_scores, query_states, precision=highest) * score_scale
    )
    value_heads = jnp.einsum("skglm,slkgd->smkgd", probabilities, grad_out, precision=highest)
    shape_now = key_heads.shape
    split_shape = (
        shape_now[0],
        shape_now[1],
        shape_now[2],
        shape_now[3] // head_block,
        head_block,
        shape_now[4],
    )
    grad_keys = jnp.sum(key_heads.reshape(split_shape), axis=4)
    grad_values = jnp.sum(value_heads.reshape(split_shape), axis=4)
    return (outputs, grad_queries, grad_keys, grad_values)


def transposed_rows(inputs, grads):
    return lax.dot_general(
        inputs, grads, (((0,), (0,)), ((), ())), preferred_element_type=jnp.float32
    )


def per_device(inputs, query_weight, kv_weight, out_grad):
    tensor_rank = lax.axis_index("tensor")
    tok_dev = inputs.shape[0]
    seqs_here = tok_dev // L
    query_cols = query_weight.shape[1]
    per_rank = query_cols // HD
    group_size = QH // KVH
    head_block = min(group_size, per_rank)
    kv_rank = per_rank // head_block
    kv_cols = kv_rank * HD
    rows_blk = query_weight.shape[0]
    first_kv = tensor_rank * per_rank // group_size
    chosen = lax.dynamic_slice_in_dim(kv_weight, first_kv * HD, kv_cols, 2)
    kv_local = jnp.concatenate([chosen[0], chosen[1]], axis=1)
    query_full = lax.all_gather(query_weight, "blk", axis=0, tiled=True)
    kv_full = lax.all_gather(kv_local, "blk", axis=0, tiled=True)
    query_states = jnp.dot(inputs, query_full, preferred_element_type=jnp.float32)
    kv_states = jnp.dot(inputs, kv_full, preferred_element_type=jnp.float32)
    query_states = rotary(query_states.reshape(seqs_here, L, per_rank, HD), 1.0).reshape(
        seqs_here, L, kv_rank, head_block, HD
    )
    key_states = rotary(kv_states[:, :kv_cols].reshape(seqs_here, L, kv_rank, HD), 1.0)
    value_states = kv_states[:, kv_cols:].reshape(seqs_here, L, kv_rank, HD)
    grad_out = out_grad.astype(jnp.float32).reshape(seqs_here, L, kv_rank, head_block, HD)
    outputs, grad_queries, grad_keys, grad_values = attend(
        query_states, key_states, value_states, grad_out, head_block
    )
    attention = outputs.reshape(tok_dev, query_cols).astype(jnp.bfloat16)
    grad_queries = (
        rotary(grad_queries.reshape(seqs_here, L, per_rank, HD), -1.0)
        .reshape(tok_dev, query_cols)
        .astype(jnp.bfloat16)
    )
    grad_keys = (
        rotary(grad_keys.reshape(seqs_here, L, kv_rank, HD), -1.0)
        .reshape(tok_dev, kv_cols)
        .astype(jnp.bfloat16)
    )
    grad_values = grad_values.reshape(tok_dev, kv_cols).astype(jnp.bfloat16)
    grad_kv = jnp.concatenate([grad_keys, grad_values], axis=1)
    query_rows_sum = lax.psum_scatter(
        transposed_rows(inputs, grad_queries).astype(jnp.bfloat16),
        "blk",
        scatter_dimension=0,
        tiled=True,
    )
    kv_rows_sum = lax.psum_scatter(
        transposed_rows(inputs, grad_kv).astype(jnp.bfloat16),
        "blk",
        scatter_dimension=0,
        tiled=True,
    ).astype(jnp.float32)
    pair_grads = jnp.stack([kv_rows_sum[:, :kv_cols], kv_rows_sum[:, kv_cols:]])
    placed = jnp.zeros((2, rows_blk, KVH * HD), jnp.float32)
    placed = lax.dynamic_update_slice(
        placed, pair_grads, (jnp.int32(0), jnp.int32(0), first_kv * HD)
    )
    kv_summed = lax.psum(placed.astype(jnp.bfloat16), "tensor")
    result = lax.dot_general(
        grad_queries, query_full, (((1,), (1,)), ((), ())), preferred_element_type=jnp.float32
    )
    grad_inputs = lax.psum_scatter(
        (
            result
            + lax.dot_general(
                grad_kv, kv_full, (((1,), (1,)), ((), ())), preferred_element_type=jnp.float32
            )
        ).astype(jnp.bfloat16),
        "tensor",
        scatter_dimension=0,
        tiled=True,
    )
    return (attention, query_rows_sum, kv_summed, grad_inputs)


def solution(mesh):
    return jax.shard_map(
        per_device,
        mesh=mesh,
        in_specs=(P("blk", None), P("blk", "tensor"), P(None, "blk", None), P("blk", "tensor")),
        out_specs=(
            P("blk", "tensor"),
            P("blk", "tensor"),
            P(None, "blk", None),
            P(("blk", "tensor"), None),
        ),
        check_vma=False,
    )
```

profile of v0, /device:TPU:1, one launch (start us, length us, event | category | flops | bytes accessed | tf_op | source)
XLA Modules:
  0.0 718.5 jit_solution(7129619898715126618)
XLA Ops:
  9.6 1.1 reshape.215
  10.7 1.3 broadcast_multiply_fusion
  12.0 90.4 %all-gather.3.cloned.1.call-done = bf16[8192,256]{1,0:T(8,128)(2,1)} async-done(((bf16[256,256]{1,0:T(8,128)(2,1)}), bf16[8192,256]{1,0:T(8,128)(2,1)}) %all-gather.3.cloned.1.call-update) | async-done | bytes 4194320 | tf_op jit(solution)/shard_map/all_gather | solution.py:96
  102.4 5.3 convolution_bitcast_fusion
  108.4 95.0 %all-gather.5.cloned.1.call-done = bf16[8192,512]{1,0:T(8,128)(2,1)} async-done(((bf16[256,512]{1,0:T(8,128)(2,1)}), bf16[8192,512]{1,0:T(8,128)(2,1)}) %all-gather.5.cloned.1.call-update) | async-done | bytes 8388624 | tf_op jit(solution)/shard_map/all_gather | solution.py:95
  203.4 7.1 fusion.42
  211.2 2.1 fusion.41
  213.6 1.8 fusion.16
  215.5 4.4 bitcast_convert_fusion
  220.6 3.1 fusion.4
  223.7 1.9 fusion.12
  225.6 0.9 subtract_convert_fusion.1
  227.3 4.3 fusion.2
  231.7 3.7 fusion.11
  236.2 9.3 %fusion = bf16[8192,512]{0,1:T(8,128)(2,1)} fusion(bf16[320,8192]{1,0:T(8,128)(2,1)} %param.4, bf16[40,8,4,128]{3,2,1,0:T(4,128)(2,1)S(1)} %bitcast.123), kind=kOutput, calls=%fused_computation.2 | convolution fusion | flops 2688548864 | bytes 13959168 | tf_op jit(solution)/shard_map/dot_general | solution.py:76
  245.6 11.8 %fusion.19 = f32[320,8192]{1,0:T(8,128)} fusion(bf16[8192,512]{1,0:T(8,128)(2,1)} %all-gather.5.cloned.1.call-done, bf16[40,8,4,128]{3,2,1,0:T(4,128)(2,1)S(1)} %bitcast.124), kind=kOutput, calls=%fused_computation.32 | convolution fusion | flops 2684354560 | bytes 19202048 | tf_op jit(solution)/shard_map/dot_general | solution.py:139
  257.3 93.5 %reduce-scatter.6.cloned.1.call-done = bf16[256,256]{0,1:T(8,128)(2,1)} async-done(((bf16[8192,256]{0,1:T(8,128)(2,1)}), bf16[256,256]{0,1:T(8,128)(2,1)}) %reduce-scatter.6.cloned.1.call-update) | async-done | bytes 131088 | tf_op jit(solution)/shard_map/reduce_scatter | solution.py:127
  352.9 9.2 %fusion.1 = bf16[320,8192]{1,0:T(8,128)(2,1)} fusion(f32[320,8192]{1,0:T(8,128)} %fusion.19, bf16[8192,256]{1,0:T(8,128)(2,1)} %all-gather.3.cloned.1.call-done, bf16[320,128]{1,0:T(8,128)(2,1)S(1)} %copy-done.12, bf16[320,128]{1,0:T(8,128)(2,1)S(1)} %copy-done.7), kind=kOutput, calls=%fused_computation.3 | convolution fusion | flops 1347747840 | bytes 20086784 | tf_op jit(solution)/shard_map/dot_general | solution.py:145
  362.1 0.9 copy-done.10
  364.0 143.8 %reduce-scatter.4.cloned.1.call-done = bf16[256,512]{0,1:T(8,128)(2,1)} async-done(((bf16[8192,512]{0,1:T(8,128)(2,1)}), bf16[256,512]{0,1:T(8,128)(2,1)}) %reduce-scatter.4.cloned.1.call-update) | async-done | bytes 262160 | tf_op jit(solution)/shard_map/reduce_scatter | solution.py:121
  507.9 1.8 copy.25
  509.7 80.2 %all-reduce.2.cloned.1.call-done = bf16[2,256,512]{2,1,0:T(8,128)(2,1)} async-done(((bf16[2,256,512]{2,1,0:T(8,128)(2,1)}), bf16[2,256,512]{2,1,0:T(8,128)(2,1)}) %all-reduce.2.cloned.1.call-update) | async-done | bytes 524304 | tf_op jit(solution)/shard_map/psum | solution.py:138
  589.9 119.9 %reduce-scatter.8.cloned.1.call-done = bf16[40,8192]{1,0:T(8,128)(2,1)} async-done(((bf16[320,8192]{1,0:T(8,128)(2,1)}), bf16[40,8192]{1,0:T(8,128)(2,1)}) %reduce-scatter.8.cloned.1.call-update) | async-done | bytes 655376 | tf_op jit(solution)/shard_map/reduce_scatter | solution.py:142
  709.7 1.9 copy.65
  (67 shorter events, 9.5 us)
Async XLA Ops:
  7.2 95.2 %all-gather.3.cloned.1.call-start = ((), (), s32[]{:S(2)}) async-start(), calls=%async_computation.3 | async-start | bytes 4325376 | tf_op jit(solution)/shard_map/all_gather | solution.py:96
  8.8 194.5 %all-gather.5.cloned.1.call-start = ((), (), s32[]{:S(2)}) async-start(), calls=%async_computation.4 | async-start | bytes 8650752 | tf_op jit(solution)/shard_map/all_gather | solution.py:95
  9.6 341.3 %reduce-scatter.6.cloned.1.call-start = ((), (), s32[]{:S(2)}) async-start(), calls=%async_computation.6 | async-start | bytes 4325376 | tf_op jit(solution)/shard_map/reduce_scatter | solution.py:127
  107.7 107.8 %copy-start.13 = (f32[320,256]{1,0:T(8,128)}, f32[320,256]{1,0:T(8,128)S(1)}, u32[]{:S(2)}) copy-start(f32[320,256]{1,0:T(8,128)S(1)} %convolution_bitcast_fusion) | copy-start | bytes 983044
  211.2 2.4 copy-start.1
  211.2 2.4 copy-start.3
  211.2 2.4 copy-start.9
  213.3 6.6 copy-start
  220.5 6.8 slice-start
  220.6 3.1 copy-start.2
  220.6 3.1 copy-start.4
  220.6 6.7 slice-start.1
  223.7 3.6 copy-start.11
  226.6 0.6 copy-start.6
  231.6 3.8 copy-start.8
  231.6 276.3 %reduce-scatter.4.cloned.1.call-start = ((), (), s32[]{:S(2)}) async-start(), calls=%async_computation.5 | async-start | bytes 8650752 | tf_op jit(solution)/shard_map/reduce_scatter | solution.py:121
  245.5 344.3 %all-reduce.2.cloned.1.call-start = ((), (), s32[]{:S(2)}) async-start(), calls=%async_computation.7 | async-start | bytes 1048576 | tf_op jit(solution)/shard_map/psum | solution.py:138
  257.3 95.5 %copy-start.7 = (bf16[320,128]{1,0:T(8,128)(2,1)S(1)}, bf16[320,128]{1,0:T(8,128)(2,1)}, u32[]{:S(2)}) copy-start(bf16[320,128]{1,0:T(8,128)(2,1)} %copy-done.6) | copy-start | bytes 245764
  257.3 95.5 %copy-start.12 = (bf16[320,128]{1,0:T(8,128)(2,1)S(1)}, bf16[320,128]{1,0:T(8,128)(2,1)}, u32[]{:S(2)}) copy-start(bf16[320,128]{1,0:T(8,128)(2,1)} %fusion.16) | copy-start | bytes 245764
  352.0 0.8 copy-start.5
  352.8 356.9 %reduce-scatter.8.cloned.1.call-start = ((), (), s32[]{:S(2)}) async-start(), calls=%async_computation.8 | async-start | bytes 5898240 | tf_op jit(solution)/shard_map/reduce_scatter | solution.py:142
  362.0 1.0 copy-start.10
Sparse Core Ops, SparseCore 0:
  11.4 91.0 all-gather.2
  105.2 98.1 all-gather.4
  231.7 119.0 reduce-scatter.5
  355.7 152.0 reduce-scatter.3
  511.1 78.7 all-reduce.1
  592.9 116.8 reduce-scatter.7
where the time goes:
time: 719 us; the launch traced here: 718 us
  waiting for transfers between devices  624 us (87%)
  matrix products  63.9 us (9%)
  between operations  14.5 us (2%)
  local copies, waits for them, and re-layouts  11.1 us (2%)
    reduce_scatter x1, waiting for transfers between devices, per_device(): lax.psum_scatter(transposed_rows(inputs, grad_queries).astype(jnp.bfloat1...  144 us
    reduce_scatter x1, waiting for transfers between devices, per_device(): lax.psum_scatter((result + lax.dot_general(grad_kv, kv_full, (((1,), (1,)...  120 us
    all_gather x1, waiting for transfers between devices, per_device(): query_full = lax.all_gather(query_weight, 'blk', axis=0, tiled=True)  95 us
    reduce_scatter x1, waiting for transfers between devices, per_device(): lax.psum_scatter(transposed_rows(inputs, grad_kv).astype(jnp.bfloat16), '...  93.5 us
    all_gather x1, waiting for transfers between devices, per_device(): kv_full = lax.all_gather(kv_local, 'blk', axis=0, tiled=True)  90.4 us
    psum x1, waiting for transfers between devices, per_device(): kv_summed = lax.psum(placed.astype(jnp.bfloat16), 'tensor')  80.2 us
  transfers between devices with their start and end apart: 6, of which 6 were waited for; matrix products, arithmetic and copies ran while one was open for 7% of the time, Pallas kernels for 0%

commit v1 on v0

v1 whole, which is shorter than its diff:
```python
import functools
import math

import jax
import jax.numpy as jnp
import numpy as np
from jax import lax
from jax.experimental import pallas as pl
from jax.experimental.pallas import tpu as pltpu
from jax.sharding import PartitionSpec as P

HD = 128
HEADS = 4
L = 320
NZ = 8
WR = 256
WC = 640
QC = 512
AF = 128
RF = 256
MESH = pl.DeviceIdType.MESH
BF = jnp.bfloat16
F32 = jnp.float32
NT = (((1,), (1,)), ((), ()))
NN = (((1,), (0,)), ((), ()))
SCALE = 1.0 / math.sqrt(HD)
SGN = (1, -1)


def dot(a, b, dims=NN):
    return lax.dot_general(a, b, dims, preferred_element_type=F32)


def kernel(
    x_hbm, w_ref, do_ref, cos_ref, sin_ref,
    att_ref, dwq_ref, dkv_ref, dx_ref,
    xv, wg, acc, kvs, kvr, gq, gkv2, gt, qh_s, pw, rc, rz, rxf, xfs, xfr,
    dxp, ry0, ry1, keep, ls, rl, kvb,
    lsem, zs, zr, xs, xr, cs, cr, es, er,
    pcs, pcr, pxs, pxr, pzs, pzr, pfs, pfr, y0s, y0r, y1s, y1r, lls, llr, ks, kr,
):
    blk = lax.axis_index("blk")
    t = lax.axis_index("tensor")
    z, h, c = blk // 4, (blk // 2) % 2, blk % 2
    y, l = t // 2, t % 2

    def dev(zz, hh, cc, yy, ll):
        return (zz * 4 + hh * 2 + cc, yy * 2 + ll)

    znb = (dev((z + 1) % NZ, h, c, y, l), dev((z + NZ - 1) % NZ, h, c, y, l))
    ynb = (dev(z, h, c, (y + 1) % 4, l), dev(z, h, c, (y + 3) % 4, l))
    xpeer = dev(z, 1 - h, c, y, l)
    cpeer = dev(z, h, 1 - c, y, l)
    lpeer = dev(z, h, c, y, 1 - l)
    tpeers = [(blk, (t + k) % 8) for k in range(1, 8)]

    sends = []

    def send(src, dst, ssem, rsem, peer):
        copy = pltpu.make_async_remote_copy(
            src_ref=src, dst_ref=dst, send_sem=ssem, recv_sem=rsem,
            device_id=peer, device_id_type=MESH,
        )
        copy.start()
        sends.append(copy)

    def arrived(ref, ssem, rsem, peer):
        pltpu.make_async_remote_copy(
            src_ref=ref, dst_ref=ref, send_sem=ssem, recv_sem=rsem,
            device_id=peer, device_id_type=MESH,
        ).wait_recv()

    xcopy = pltpu.make_async_copy(x_hbm, xv, lsem.at[0])
    xcopy.start()
    own = h * 2 + c
    oth = (1 - h) * 2 + c
    wg[z, own] = w_ref[...]

    barrier = pltpu.get_barrier_semaphore()
    greet = [znb[0], znb[1], xpeer, cpeer] + tpeers
    for peer in greet:
        pl.semaphore_signal(barrier, inc=1, device_id=peer, device_id_type=MESH)
    pl.semaphore_wait(barrier, len(greet))

    def slot(d, k):
        return (z + 2 * NZ - SGN[k] * d) % NZ

    def own_rows(d, k):
        return pl.ds(0, WR) if d < 4 else pl.ds(k * (WR // 2), WR // 2)

    half = (WR - AF) // 2

    def oth_rows(d, k):
        if d == 0:
            return pl.ds(0, WR)
        return pl.ds(AF, WR - AF) if d < 4 else pl.ds(AF + k * half, half)

    def proj(zp):
        xcols = xv[:, pl.ds(pl.multiple_of(zp * 1024, 1024), 1024)]
        acc[...] += dot(xcols, wg[zp].reshape(4 * WR, WC))

    for k in (0, 1):
        send(wg.at[z, own], wg.at[z, own], zs.at[0, k, 1], zr.at[0, k, 1], znb[k])
    send(wg.at[z, own], wg.at[z, own], xs.at[0, 0], xr.at[0, 0], xpeer)
    send(wg.at[z, own], wg.at[z, own], cs.at[0, 0, 0], cr.at[0, 0, 0], cpeer)
    acc[...] = jnp.zeros_like(acc)
    arrived(wg.at[z, oth], xs.at[0, 0], xr.at[0, 0], xpeer)
    for k in (0, 1):
        part = wg.at[z, oth, oth_rows(1, k)]
        send(part, part, zs.at[1, k, 1], zr.at[1, k, 1], znb[k])
    send(wg.at[z, oth], wg.at[z, oth], cs.at[1, 0, 0], cr.at[1, 0, 0], cpeer)

    def tick(d, k):
        zp = slot(d, k)
        for ring, hc, rows in ((0, own, own_rows), (1, oth, oth_rows)):
            here = wg.at[zp, hc, rows(d, k)]
            arrived(here, zs.at[ring, k, d], zr.at[ring, k, d], znb[1 - k])
            if d < 4:
                part = wg.at[zp, hc, rows(d + 1, k)]
                send(part, part, zs.at[ring, k, d + 1], zr.at[ring, k, d + 1], znb[k])
            if ring == 0 and (d < 4 or k == 0):
                part = wg.at[zp, hc, pl.ds(0, AF)]
                send(part, part, xs.at[k, d], xr.at[k, d], xpeer)
            send(here, here, cs.at[ring, k, d], cr.at[ring, k, d], cpeer)

    def from_x(d, k):
        part = wg.at[slot(d, k), oth, pl.ds(0, AF)]
        arrived(part, xs.at[k, d], xr.at[k, d], xpeer)
        send(part, part, cs.at[2, k, d], cr.at[2, k, d], cpeer)

    def from_core(d, k):
        zp = slot(d, k)
        part = wg.at[zp, h * 2 + 1 - c, own_rows(d, k)]
        arrived(part, cs.at[0, k, d], cr.at[0, k, d], cpeer)
        part = wg.at[zp, (1 - h) * 2 + 1 - c, oth_rows(d, k)]
        arrived(part, cs.at[1, k, d], cr.at[1, k, d], cpeer)
        if 0 < d and (d < 4 or k == 0):
            part = wg.at[zp, (1 - h) * 2 + 1 - c, pl.ds(0, AF)]
            arrived(part, cs.at[2, k, d], cr.at[2, k, d], cpeer)

    tick(1, 0)
    tick(1, 1)
    xcopy.wait()
    from_core(0, 0)
    proj(z)
    tick(2, 0)
    tick(2, 1)
    from_x(1, 0)
    from_x(1, 1)
    for k in (0, 1):
        from_core(1, k)
        proj(slot(1, k))
    tick(3, 0)
    tick(3, 1)
    from_x(2, 0)
    from_x(2, 1)
    for k in (0, 1):
        from_core(2, k)
        proj(slot(2, k))
    tick(4, 0)
    tick(4, 1)
    from_x(3, 0)
    from_x(3, 1)
    for k in (0, 1):
        from_core(3, k)
        proj(slot(3, k))
    from_x(4, 0)
    from_core(4, 0)
    from_core(4, 1)
    proj(slot(4, 0))

    kvs[...] = acc[:, QC:]
    send(kvs, kvr, es.at[0], er.at[0], lpeer)

    cosv = cos_ref[...]
    sinv = sin_ref[...]

    def rot(v):
        return v * cosv + pltpu.roll(v, HD // 2, 1) * sinv

    def unrot(v):
        return v * cosv - pltpu.roll(v, HD // 2, 1) * sinv

    for g in range(HEADS):
        qr = rot(acc[:, pl.ds(g * HD, HD)])
        acc[:, pl.ds(g * HD, HD)] = qr * SCALE
        qh_s[g] = qr.astype(BF)

    arrived(kvr, es.at[0], er.at[0], lpeer)
    first = l == 0
    mine, other = kvs[...], kvr[...]
    kr_f = rot(jnp.where(first, mine, other))
    kh = kr_f.astype(BF)
    kl = (kr_f - kh.astype(F32)).astype(BF)
    vb = jnp.where(first, other, mine).astype(BF)
    kcat = jnp.concatenate([kh, kl, kh], axis=1)
    allowed = lax.broadcasted_iota(jnp.int32, (L, L), 1) <= lax.broadcasted_iota(
        jnp.int32, (L, L), 0
    )
    dk = jnp.zeros((L, HD), F32)
    dv = jnp.zeros((L, HD), F32)
    for g in range(HEADS):
        cols = pl.ds(g * HD, HD)
        qs = acc[:, cols]
        qsh = qs.astype(BF)
        qsl = (qs - qsh.astype(F32)).astype(BF)
        s = dot(jnp.concatenate([qsh, qsh, qsl], axis=1), kcat, NT)
        s = jnp.where(allowed, s, -1e30)
        e = jnp.exp(s - jnp.max(s, axis=1, keepdims=True))
        p = e / jnp.sum(e, axis=1, keepdims=True)
        pb = p.astype(BF)
        dob = do_ref[:, cols]
        att_ref[:, cols] = dot(pb, vb).astype(BF)
        dp = dot(dob, vb, NT)
        ds = p * (dp - jnp.sum(p * dp, axis=1, keepdims=True))
        dsb = ds.astype(BF)
        dq = unrot(dot(dsb, kh) * SCALE)
        gq[:, cols] = dq.astype(BF)
        gt[cols, :] = dq.T.astype(BF)
        dk = dk + dot(dsb.T, qh_s[g])
        dv = dv + dot(pb.T, dob)
    dk = unrot(dk * SCALE)
    gkv2[0] = jnp.where(first, dk, dv).astype(BF)
    gkv2[1] = jnp.where(first, dv, dk).astype(BF)
    send(gkv2.at[1], gkv2.at[2], es.at[1], er.at[1], lpeer)
    gt[pl.ds(QC, HD), :] = gkv2[0].astype(F32).T.astype(BF)
    arrived(gkv2.at[2], es.at[1], er.at[1], lpeer)
    gt[pl.ds(WC, HD), :] = gkv2[2].astype(F32).T.astype(BF)

    def add(dst, src, rows, n, step):
        base = 0 if rows is None else rows

        def body(i, carry):
            r = pl.ds(pl.multiple_of(base + i * step, 16), step)
            dst[r, :] = dst[r, :] + src[r, :]
            return carry

        lax.fori_loop(0, n // step, body, 0)

    def zat(o):
        return (z + NZ + o) % NZ

    def products(o):
        zp = zat(o)

        def body(j, carry):
            xcols = xv[:, pl.ds(pl.multiple_of(zp * 1024 + j * WR, WR), WR)]
            cc, hh = j % 2, j // 2
            pw[zp, cc, hh, pl.ds(0, QC), :] = dot(gt[pl.ds(0, QC), :], xcols).astype(BF)
            both = dot(gt[pl.ds(QC, HD), :], xcols) + dot(gt[pl.ds(WC, HD), :], xcols)
            pw[zp, cc, hh, pl.ds(QC, HD), :] = both.astype(BF)
            return carry

        lax.fori_loop(0, 4, body, 0)
        i = o % NZ
        send(pw.at[zp, 1 - c], rc.at[i], pcs.at[i], pcr.at[i], cpeer)

    def core_sum(o):
        zp, i = zat(o), o % NZ
        arrived(rc.at[i], pcs.at[i], pcr.at[i], cpeer)
        for hh in (0, 1):
            add(pw.at[zp, c, hh], rc.at[i, hh], None, WC, 128)
        part = pw.at[zp, c, 1 - h, pl.ds(0, RF)]
        send(part, rxf.at[i], pxs.at[i], pxr.at[i], xpeer)

    def x_sum(o):
        zp, i = zat(o), o % NZ
        arrived(rxf.at[i], pxs.at[i], pxr.at[i], xpeer)
        add(pw.at[zp, c, h], rxf.at[i], None, RF, 128)

    mid = (WC - RF) // 2

    def z_rows(s, ring, k):
        if ring == 0:
            return (0, WC) if s > 0 else (k * (WC // 2), WC // 2)
        return (RF, WC - RF) if s > 0 else (RF + k * mid, mid)

    def z_step(s, ring, k):
        hh = h if ring == 0 else 1 - h
        zp = zat(SGN[k] * (4 - s))
        if s > 0:
            base, n = z_rows(s - 1, ring, k)
            src = rz.at[s - 1, ring, k]
            arrived(
                src.at[pl.ds(base, n)], pzs.at[s - 1, ring, k], pzr.at[s - 1, ring, k],
                znb[1 - k],
            )
            add(pw.at[zp, c, hh], src, base, n, 64)
        base, n = z_rows(s, ring, k)
        send(
            pw.at[zp, c, hh, pl.ds(base, n)], rz.at[s, ring, k, pl.ds(base, n)],
            pzs.at[s, ring, k], pzr.at[s, ring, k], znb[k],
        )

    def z_last(ring):
        base, n = z_rows(3, ring, 0)
        for k in (0, 1):
            arrived(
                rz.at[3, ring, k, pl.ds(base, n)], pzs.at[3, ring, k], pzr.at[3, ring, k],
                znb[1 - k],
            )

    def dx_products(i):
        for hf in (0, 1):
            w = wg[i, 2 * hf:2 * hf + 2].reshape(2 * WR, WC)
            wkv = w[:, QC:]
            r = dot(gq[...], w[:, :QC], NT) + dot(gkv2[0], wkv, NT) + dot(gkv2[2], wkv, NT)
            dxp[i, :, hf] = r.reshape(4, 80, 512).astype(BF)
        for k in (0, 1):
            send(
                dxp.at[i, (y + 2) % 4, k], ry0.at[i, k], y0s.at[i, k], y0r.at[i, k], ynb[k]
            )

    def y_step(i):
        for k in (0, 1):
            arrived(ry0.at[i, k], y0s.at[i, k], y0r.at[i, k], ynb[1 - k])
            yy = (y + 4 + SGN[k]) % 4
            dxp[i, yy, k] = dxp[i, yy, k] + ry0[i, k]
            send(dxp.at[i, yy], ry1.at[i, k], y1s.at[i, k], y1r.at[i, k], ynb[k])

    def y_last(i):
        for k in (0, 1):
            arrived(ry1.at[i, k], y1s.at[i, k], y1r.at[i, k], ynb[1 - k])
        s = dxp[i, y].astype(F32) + ry1[i, 0].astype(F32) + ry1[i, 1].astype(F32)
        a = jnp.concatenate([s[0, :40], s[1, :40]], axis=0)
        b = jnp.concatenate([s[0, 40:], s[1, 40:]], axis=0)
        keep[i] = jnp.where(first, a, b)
        ls[i] = jnp.where(first, b, a).astype(BF)
        send(ls.at[i], rl.at[i], lls.at[i], llr.at[i], lpeer)

    def l_last(i):
        arrived(rl.at[i], lls.at[i], llr.at[i], lpeer)
        s = (keep[i] + rl[i].astype(F32)).astype(BF)
        dx_ref[:, pl.ds(i * 1024, 512)] = s[:40]
        dx_ref[:, pl.ds(i * 1024 + 512, 512)] = s[40:]

    def z_both(s, ring):
        z_step(s, ring, 0)
        z_step(s, ring, 1)

    products(4)
    products(3)
    products(-3)
    dx_products(0)
    core_sum(4)
    z_both(0, 1)
    dx_products(1)
    core_sum(3)
    core_sum(-3)
    products(2)
    products(-2)
    x_sum(4)
    z_both(0, 0)
    dx_products(2)
    dx_products(3)
    x_sum(3)
    x_sum(-3)
    core_sum(2)
    core_sum(-2)
    y_step(0)
    y_step(1)
    z_both(1, 1)
    products(1)
    products(-1)
    dx_products(4)
    z_both(1, 0)
    x_sum(2)
    x_sum(-2)
    core_sum(1)
    core_sum(-1)
    dx_products(5)
    y_step(2)
    products(0)
    dx_products(6)
    y_step(3)
    core_sum(0)
    z_both(2, 1)
    z_both(2, 0)
    dx_products(7)
    y_step(4)
    y_step(5)
    y_last(0)
    x_sum(1)
    x_sum(-1)
    x_sum(0)
    y_step(6)
    y_last(1)
    y_last(2)
    z_both(3, 1)
    z_both(3, 0)
    y_step(7)
    for i in range(3, 8):
        y_last(i)
        l_last(i - 3)

    zc = (z, c)
    z_last(1)
    for r in range(RF, WC, 128):
        rows = pl.ds(r, 128)
        xfs[pl.ds(r - RF, 128), :] = (
            pw[z, c, 1 - h, rows, :].astype(F32)
            + rz[3, 1, 0, rows, :].astype(F32)
            + rz[3, 1, 1, rows, :].astype(F32)
        ).astype(BF)
    send(xfs, xfr, pfs.at[0], pfr.at[0], xpeer)
    z_last(0)

    def total(r):
        rows = pl.ds(r, 128)
        s = (
            pw[z, c, h, rows, :].astype(F32)
            + rz[3, 0, 0, rows, :].astype(F32)
            + rz[3, 0, 1, rows, :].astype(F32)
        )
        if r >= RF:
            s = s + xfr[pl.ds(r - RF, 128), :].astype(F32)
        return s.T.astype(BF)

    for r in range(0, RF, 128):
        dwq_ref[:, pl.ds(r, 128)] = total(r)
    arrived(xfr, pfs.at[0], pfr.at[0], xpeer)
    kvb[t] = total(QC)
    for k, peer in enumerate(tpeers):
        send(kvb.at[t], kvb.at[t], ks.at[k], kr.at[t], peer)
    for r in range(RF, QC, 128):
        dwq_ref[:, pl.ds(r, 128)] = total(r)
    for i in range(5, 8):
        l_last(i)
    for k, peer in enumerate(tpeers):
        tt = (t + 1 + k) % 8
        arrived(kvb.at[tt], ks.at[k], kr.at[tt], peer)
    for yy in range(4):
        for ll in range(2):
            dkv_ref[ll, :, pl.ds(yy * HD, HD)] = kvb[yy * 2 + ll]
    for copy in sends:
        copy.wait_send()


def tables():
    i = np.arange(HD // 2, dtype=np.float64)
    ang = np.arange(L, dtype=np.float64)[:, None] * np.exp(i * (-2.0 * math.log(10000.0) / HD))
    cos, sin = np.cos(ang), np.sin(ang)
    return (
        np.concatenate([cos, cos], axis=1).astype(np.float32),
        np.concatenate([-sin, sin], axis=1).astype(np.float32),
    )


def per_device(inputs, query_weight, kv_weight, out_grad):
    t = lax.axis_index("tensor")
    kv = lax.dynamic_slice(kv_weight, (t % 2, 0, (t // 2) * HD), (1, WR, HD))[0]
    w = jnp.concatenate([query_weight, kv], axis=1)
    cos, sin = tables()
    vm = pl.BlockSpec(memory_space=pltpu.VMEM)
    dma = pltpu.SemaphoreType.DMA
    return pl.pallas_call(
        kernel,
        out_shape=(
            jax.ShapeDtypeStruct((L, QC), BF),
            jax.ShapeDtypeStruct((WR, QC), BF),
            jax.ShapeDtypeStruct((2, WR, QC), BF),
            jax.ShapeDtypeStruct((40, 8192), BF),
        ),
        in_specs=[pl.BlockSpec(memory_space=pl.ANY), vm, vm, vm, vm],
        out_specs=(vm, vm, vm, vm),
        scratch_shapes=[
            pltpu.VMEM((L, 8192), BF),
            pltpu.VMEM((NZ, 4, WR, WC), BF),
            pltpu.VMEM((L, WC), F32),
            pltpu.VMEM((L, HD), F32),
            pltpu.VMEM((L, HD), F32),
            pltpu.VMEM((L, QC), BF),
            pltpu.VMEM((3, L, HD), BF),
            pltpu.VMEM((WC + HD, L), BF),
            pltpu.VMEM((HEADS, L, HD), BF),
            pltpu.VMEM((NZ, 2, 2, WC, WR), BF),
            pltpu.VMEM((NZ, 2, WC, WR), BF),
            pltpu.VMEM((4, 2, 2, WC, WR), BF),
            pltpu.VMEM((NZ, RF, WR), BF),
            pltpu.VMEM((WC - RF, WR), BF),
            pltpu.VMEM((WC - RF, WR), BF),
            pltpu.VMEM((8, 4, 2, 80, 512), BF),
            pltpu.VMEM((8, 2, 80, 512), BF),
            pltpu.VMEM((8, 2, 2, 80, 512), BF),
            pltpu.VMEM((8, 80, 512), F32),
            pltpu.VMEM((8, 80, 512), BF),
            pltpu.VMEM((8, 80, 512), BF),
            pltpu.VMEM((8, WR, HD), BF),
            dma((1,)),
            dma((2, 2, 5)), dma((2, 2, 5)),
            dma((2, 5)), dma((2, 5)),
            dma((3, 2, 5)), dma((3, 2, 5)),
            dma((2,)), dma((2,)),
            dma((8,)), dma((8,)),
            dma((8,)), dma((8,)),
            dma((4, 2, 2)), dma((4, 2, 2)),
            dma((1,)), dma((1,)),
            dma((8, 2)), dma((8, 2)),
            dma((8, 2)), dma((8, 2)),
            dma((8,)), dma((8,)),
            dma((7,)), dma((8,)),
        ],
        compiler_params=pltpu.CompilerParams(
            collective_id=0, has_side_effects=True, vmem_limit_bytes=60 * 2**20
        ),
        cost_estimate=pl.CostEstimate(
            flops=14_000_000_000, bytes_accessed=8_000_000, transcendentals=410_000
        ),
        name="attention_step",
    )(inputs, w, out_grad, cos, sin)


def solution(mesh):
    return jax.shard_map(
        per_device,
        mesh=mesh,
        in_specs=(P("blk", None), P("blk", "tensor"), P(None, "blk", None), P("blk", "tensor")),
        out_specs=(
            P("blk", "tensor"),
            P("blk", "tensor"),
            P(None, "blk", None),
            P(("blk", "tensor"), None),
        ),
        check_vma=False,
    )
```

time: 719 us -> 155 us (0.22)
  waiting for transfers between devices: 624 us -> 0 us
  Pallas kernels: 0 us -> 145 us
  matrix products: 63.9 us -> 0 us
  between operations: 14.5 us -> 0.68 us
    reduce_scatter x3 -> x0, waiting for transfers between devices: 357 us -> none  [the longest x1 144 us: per_device(): lax.psum_scatter(transposed_rows(inputs, grad_queries).astype(jnp.bfloat1...]
    all_gather x2 -> x0, waiting for transfers between devices: 185 us -> none  [the longest x1 95 us: per_device(): query_full = lax.all_gather(query_weight, 'blk', axis=0, tiled=True)]
    pallas_call x0 -> x1, Pallas kernels: none -> 145 us  [per_device(): pl.pallas_call(kernel, out_shape=(jax.ShapeDtypeStruct((L, QC), BF), jax....]
    psum x1 -> x0, waiting for transfers between devices: 80.2 us -> none  [per_device(): kv_summed = lax.psum(placed.astype(jnp.bfloat16), 'tensor')]
    dot_general x12 -> x0, matrix products: 63.9 us -> none  [the longest x2 13.6 us: transposed_rows(): lax.dot_general(inputs, grads, (((0,), (0,)), ((), ())), preferred_elemen...]
  transfers between devices with their start and end apart: 6 -> 0, of which waited for: 6 -> 0; matrix products, arithmetic and copies ran while one was open for 7% -> 0% of each run, Pallas kernels for 0% -> 0%
where the time goes in v1:
time: 155 us
  Pallas kernels  145 us (94%)
  local copies, waits for them, and re-layouts  8.24 us (5%)
  other arithmetic  1.7 us (1%)
    pallas_call x1, Pallas kernels, per_device(): pl.pallas_call(kernel, out_shape=(jax.ShapeDtypeStruct((L, QC), BF), jax....  145 us
    unnamed x6, local copies, waits for them, and re-layouts  8.23 us

profile of v1, /device:TPU:1, one launch (start us, length us, event | category | flops | bytes accessed | tf_op | source)
XLA Modules:
  0.0 155.1 jit_solution(15947767940624485395)
XLA Ops:
  0.6 0.0 copy-start
  0.7 1.0 copy-done
  1.7 1.7 %pad_maximum_fusion.w_ref = bf16[256,640]{1,0:T(8,128)(2,1)} fusion(bf16[256,128]{1,0:T(8,128)(2,1)S(1)} %dynamic-slice_bitcast_fusion, bf16[256,512]{1,0:T(8,128)(2,1)} %param.7), kind=kLoop, calls=%fused_computation | loop fusion | flops 655360 | bytes 655360 | tf_op jit(solution)/shard_map/concatenate | solution.py:452
  3.4 144.5 %attention_step.1 = (bf16[320,512]{1,0:T(8,128)(2,1)}, bf16[256,512]{1,0:T(8,128)(2,1)}, bf16[2,256,512]{2,1,0:T(8,128)(2,1)}, bf16[40,8192]{1,0:T(8,128)(2,1)}) custom-call(bf16[320,8192]{1,0:T(8,128)(2,1)} %x_hbm.1, bf16[256,640]{1,0:T(8,128)(2,1)} %pad_maximum_fusion.w_ref, bf16[320,512]{1,0:T(8,128)(2,1)} %do_ref.1, f32[320,128]{1,0:T(8,128)} %constant.37.clone.cos_ref, ...), custom_call_target="tpu_custom_call" | custom-call | flops 14000000000 | bytes 8000000 | tf_op jit(solution)/shard_map/attention_step/pallas_call | solution.py:456
  147.9 1.7 %copy.14 = bf16[320,512]{1,0:T(8,128)(2,1)} copy(bf16[320,512]{1,0:T(8,128)(2,1)} %get-tuple-element.8) | data formatting | bytes 655360
  149.6 1.7 %copy.15 = bf16[256,512]{1,0:T(8,128)(2,1)} copy(bf16[256,512]{1,0:T(8,128)(2,1)} %get-tuple-element.9) | data formatting | bytes 524288
  151.3 1.9 %copy.16 = bf16[2,256,512]{2,1,0:T(8,128)(2,1)} copy(bf16[2,256,512]{2,1,0:T(8,128)(2,1)} %get-tuple-element.10) | data formatting | bytes 1048576
  153.2 2.0 %copy.17 = bf16[40,8192]{1,0:T(8,128)(2,1)} copy(bf16[40,8192]{1,0:T(8,128)(2,1)} %get-tuple-element.11) | data formatting | bytes 1310720
  (1 shorter events, 0.0 us)
Async XLA Ops:
  0.6 1.0 copy-start

commit v2 on v1

v2 whole, which is shorter than its diff:
```python
import functools
import math

import jax
import jax.numpy as jnp
import numpy as np
from jax import lax
from jax.experimental import pallas as pl
from jax.experimental.pallas import tpu as pltpu
from jax.sharding import PartitionSpec as P

HD = 128
HEADS = 4
L = 320
NZ = 8
WR = 256
WC = 640
QC = 512
AF = 160
C1 = 384
RF = 256
MESH = pl.DeviceIdType.MESH
BF = jnp.bfloat16
F32 = jnp.float32
NT = (((1,), (1,)), ((), ()))
NN = (((1,), (0,)), ((), ()))
SCALE = 1.0 / math.sqrt(HD)
SGN = (1, -1)


PLAN = (
    ("P", 4), ("D", 0), ("P", 3), ("D", 1), ("P", -3), ("S", 4), ("Z", 0, "O", 0),
    ("Z", 0, "O", 1), ("Z", 0, "N", 0), ("Z", 0, "N", 1), ("S", 3), ("Y", 0, 0), ("Y", 0, 1),
    ("D", 2), ("P", 2), ("S", -3), ("Y", 1, 0), ("Y", 1, 1), ("D", 3), ("Z", 1, "O", 0),
    ("Z", 1, "O", 1), ("A", 4), ("Z", 0, "K", 0), ("Z", 0, "K", 1), ("Z", 0, "X", 0),
    ("Z", 0, "X", 1), ("S", 2), ("Z", 1, "N", 0), ("Z", 1, "N", 1), ("YL", 0), ("P", -2),
    ("A", 3), ("Y", 2, 0), ("Y", 2, 1), ("D", 4), ("P", 1), ("D", 5), ("Z", 2, "O", 0), ("A", -3),
    ("S", -2), ("Z", 1, "K", 0), ("Z", 1, "K", 1), ("Z", 1, "X", 0), ("Z", 1, "X", 1),
    ("Z", 2, "O", 1), ("YL", 1), ("A", 2), ("S", 1), ("Y", 3, 0), ("Y", 3, 1), ("LL", 0),
    ("P", -1), ("D", 6), ("P", 0), ("Z", 2, "N", 0), ("Z", 2, "N", 1), ("A", -2), ("YL", 2),
    ("Z", 2, "K", 1), ("S", -1), ("Y", 4, 0), ("Y", 4, 1), ("LL", 1), ("D", 7), ("Z", 2, "X", 1),
    ("A", 1), ("S", 0), ("Z", 3, "O", 0), ("Y", 5, 0), ("Y", 5, 1), ("LL", 2), ("Z", 2, "K", 0),
    ("Z", 2, "X", 0), ("Z", 3, "O", 1), ("YL", 3), ("A", -1), ("Y", 6, 0), ("Y", 6, 1), ("A", 0),
    ("Z", 3, "N", 0), ("Z", 3, "N", 1), ("LL", 3), ("YL", 4), ("Z", 3, "K", 1), ("Z", 3, "X", 1),
    ("Y", 7, 0), ("Y", 7, 1), ("Z", 3, "K", 0), ("LL", 4), ("YL", 5), ("Z", 3, "X", 0),
    ("ZL", "O"), ("YL", 6), ("LL", 5), ("ZL", "K"), ("YL", 7), ("ZL", "X"), ("ZL", "N"),
    ("LL", 6), ("LL", 7), ("FIN",),
)


def dot(a, b, dims=NN):
    return lax.dot_general(a, b, dims, preferred_element_type=F32)


def kernel(
    x_hbm, wq_hbm, kv_hbm, do_hbm, cos_hbm, sin_hbm,
    att_ref, dwq_ref, dkv_ref, dx_ref,
    do_ref, cos_ref, sin_ref, xv, wg1, wg2, acc, kvs, kvr, g1, g2, gother, gsend, gt,
    qh_s, qcat, kcat, vb_s, ds_s, dk_s, dv_s, pw, rc, rz, rxf, xfs, xfr,
    dxp, ry0, ry1, keep, ls, rl, kvb,
    lsem, zs, zr, xs, xr, cs, cr, es, er,
    pcs, pcr, pxs, pxr, pzs, pzr, pfs, pfr, y0s, y0r, y1s, y1r, lls, llr, ks, kr,
):
    blk = lax.axis_index("blk")
    t = lax.axis_index("tensor")
    z, h, c = blk // 4, (blk // 2) % 2, blk % 2
    y, l = t // 2, t % 2

    def dev(zz, hh, cc, yy, ll):
        return (zz * 4 + hh * 2 + cc, yy * 2 + ll)

    znb = (dev((z + 1) % NZ, h, c, y, l), dev((z + NZ - 1) % NZ, h, c, y, l))
    ynb = (dev(z, h, c, (y + 1) % 4, l), dev(z, h, c, (y + 3) % 4, l))
    xpeer = dev(z, 1 - h, c, y, l)
    cpeer = dev(z, h, 1 - c, y, l)
    lpeer = dev(z, h, c, y, 1 - l)
    tpeers = [(blk, (t + k) % 8) for k in range(1, 8)]

    sends = []

    def send(src, dst, ssem, rsem, peer):
        copy = pltpu.make_async_remote_copy(
            src_ref=src, dst_ref=dst, send_sem=ssem, recv_sem=rsem,
            device_id=peer, device_id_type=MESH,
        )
        copy.start()
        sends.append(copy)

    def arrived(ref, ssem, rsem, peer):
        pltpu.make_async_remote_copy(
            src_ref=ref, dst_ref=ref, send_sem=ssem, recv_sem=rsem,
            device_id=peer, device_id_type=MESH,
        ).wait_recv()

    own = h * 2 + c
    oth = (1 - h) * 2 + c
    loads = [
        pltpu.make_async_copy(src, dst, lsem.at[i])
        for i, (src, dst) in enumerate((
            (wq_hbm.at[:, pl.ds(0, C1 - HD)], wg1.at[z, own, :, pl.ds(HD, C1 - HD)]),
            (wq_hbm.at[:, pl.ds(C1 - HD, WC - C1)], wg2.at[z, own]),
            (
                kv_hbm.at[l, :, pl.ds(pl.multiple_of(y * HD, HD), HD)],
                wg1.at[z, own, :, pl.ds(0, HD)],
            ),
            (x_hbm, xv),
            (do_hbm, do_ref),
            (cos_hbm, cos_ref),
            (sin_hbm, sin_ref),
        ))
    ]
    for copy in loads:
        copy.start()

    barrier = pltpu.get_barrier_semaphore()
    greet = [znb[0], znb[1], xpeer, cpeer] + tpeers
    for peer in greet:
        pl.semaphore_signal(barrier, inc=1, device_id=peer, device_id_type=MESH)
    acc[...] = jnp.zeros_like(acc)
    for copy in loads[:3]:
        copy.wait()
    pl.semaphore_wait(barrier, len(greet))

    def slot(d, k):
        return (z + 2 * NZ - SGN[k] * d) % NZ

    piece = {"A": 0, "B": 1, "O": 2, "X": 3}
    column = {"A": own, "B": own, "O": oth, "X": oth}

    class Gather:
        def __init__(self, g, buf, split, low, width):
            self.g, self.buf, self.split = g, buf, split
            self.cols = pl.ds(low, width)

        def rows(self, p, d, k):
            f = self.split
            if p in "AX":
                return pl.ds(0, f) if f > 0 and (d < 4 or k == 0) else None
            n = WR - f
            if d < 4:
                return pl.ds(f, n)
            if p == "B" and f > 0:
                return pl.ds(f, n) if k == 1 else None
            return pl.ds(f + k * (n // 2), n // 2)

        def part(self, p, d, k):
            r = self.rows(p, d, k)
            return None if r is None else self.buf.at[slot(d, k), column[p], r]

        def z_send(self, p, d, k):
            r = self.rows(p, d, k)
            if r is not None:
                ref = self.buf.at[slot(d - 1, k), column[p], r]
                at = (self.g, piece[p], k, d)
                send(ref, ref, zs.at[at], zr.at[at], znb[k])

        def x_send(self, p, d, k, ref):
            at = (self.g, piece[p], k, d)
            send(ref, ref, xs.at[at], xr.at[at], xpeer)

        def to_core(self, p, d, k, ref):
            at = (self.g, piece[p], k, d)
            send(ref, ref, cs.at[at], cr.at[at], cpeer)

        def start(self):
            for p in "AB":
                ref = self.part(p, 0, 0)
                if ref is not None:
                    for k in (0, 1):
                        self.z_send(p, 1, k)

        def start_x(self):
            for p in "BA":
                ref = self.part(p, 0, 0)
                if ref is not None:
                    self.x_send(p, 0, 0, ref)
                    self.to_core(p, 0, 0, ref)

        def start_other(self):
            ref = self.part("O", 0, 0)
            at = (self.g, 1, 0, 0)
            arrived(ref, xs.at[at], xr.at[at], xpeer)
            for k in (0, 1):
                self.z_send("O", 1, k)
            self.to_core("O", 0, 0, ref)

        def tick(self, p, d):
            for k in (0, 1):
                ref = self.part(p, d, k)
                if ref is None:
                    continue
                at = (self.g, piece[p], k, d)
                arrived(ref, zs.at[at], zr.at[at], znb[1 - k])
                if d < 4:
                    self.z_send(p, d + 1, k)
                if p == "A":
                    self.x_send("A", d, k, ref)
                self.to_core(p, d, k, ref)

        def from_x(self, d):
            for k in (0, 1):
                ref = self.part("X", d, k)
                if ref is not None and (d > 0 or k == 0):
                    at = (self.g, 0, k, d)
                    arrived(ref, xs.at[at], xr.at[at], xpeer)
                    self.to_core("X", d, k, ref)

        def from_core(self, d, k):
            zp = slot(d, k)
            for p, hc in (("A", h * 2), ("B", h * 2), ("O", 2 - h * 2), ("X", 2 - h * 2)):
                r = self.rows(p, d, k)
                if r is not None:
                    at = (self.g, piece[p], k, d)
                    arrived(self.buf.at[zp, hc + 1 - c, r], cs.at[at], cr.at[at], cpeer)

        def proj(self, d, k):
            self.from_core(d, k)
            if d == 4:
                self.from_core(d, 1 - k)
            zp = slot(d, k)
            xcols = xv[:, pl.ds(pl.multiple_of(zp * 1024, 1024), 1024)]
            w = self.buf[zp]
            acc[:, self.cols] += dot(xcols, w.reshape(4 * WR, w.shape[-1]))

    one = Gather(0, wg1, AF, 0, C1)
    two = Gather(1, wg2, 0, C1, WC - C1)

    one.start()
    one.start_x()
    one.start_other()
    one.tick("A", 1)
    one.from_x(0)
    one.tick("B", 1)
    two.start_x()
    loads[3].wait()
    one.proj(0, 0)
    one.tick("O", 1)
    for d in (2, 3):
        one.tick("A", d)
        one.from_x(d - 1)
        one.tick("B", d)
        one.proj(d - 1, 0)
        one.tick("O", d)
        one.proj(d - 1, 1)
    two.start()
    two.start_other()
    one.tick("A", 4)
    one.from_x(3)
    one.tick("B", 4)
    one.proj(3, 0)
    one.tick("O", 4)
    one.proj(3, 1)
    two.tick("B", 1)
    two.tick("O", 1)
    one.from_x(4)
    one.proj(4, 0)

    kvs[...] = acc[:, :HD]
    send(kvs, kvr, es.at[0], er.at[0], lpeer)
    for copy in loads[4:]:
        copy.wait()
    cosv = cos_ref[...]
    sinv = sin_ref[...]

    def rot(v):
        return v * cosv + pltpu.roll(v, HD // 2, 1) * sinv

    def unrot(v):
        return v * cosv - pltpu.roll(v, HD // 2, 1) * sinv

    def queries(g):
        qr = rot(acc[:, pl.ds(HD + g * HD, HD)])
        qs = qr * SCALE
        qsh = qs.astype(BF)
        qcat[g, :, pl.ds(0, HD)] = qsh
        qcat[g, :, pl.ds(HD, HD)] = (qs - qsh.astype(F32)).astype(BF)
        qh_s[g] = qr.astype(BF)

    two.proj(0, 0)
    two.tick("B", 2)
    two.tick("O", 2)
    queries(0)
    queries(1)
    two.proj(1, 0)
    two.proj(1, 1)
    two.tick("B", 3)
    two.tick("O", 3)
    arrived(kvr, es.at[0], er.at[0], lpeer)
    first = l == 0
    kr_f = rot(jnp.where(first, kvs[...], kvr[...]))
    kh = kr_f.astype(BF)
    kcat[:, pl.ds(0, HD)] = kh
    kcat[:, pl.ds(HD, HD)] = (kr_f - kh.astype(F32)).astype(BF)
    vb_s[...] = jnp.where(first, kvr[...], kvs[...]).astype(BF)

    def head(g):
        cols = pl.ds(g * HD, HD)
        vb = vb_s[...]
        qsh, qsl = qcat[g, :, :HD], qcat[g, :, HD:]
        khv, klv = kcat[:, :HD], kcat[:, HD:]
        s = dot(
            jnp.concatenate([qsh, qsh, qsl], axis=1),
            jnp.concatenate([khv, klv, khv], axis=1), NT,
        )
        allowed = lax.broadcasted_iota(jnp.int32, (L, L), 1) <= lax.broadcasted_iota(
            jnp.int32, (L, L), 0
        )
        s = jnp.where(allowed, s, -1e30)
        e = jnp.exp(s - jnp.max(s, axis=1, keepdims=True))
        p = e / jnp.sum(e, axis=1, keepdims=True)
        pb = p.astype(BF)
        dob = do_ref[:, cols]
        att_ref[:, cols] = dot(pb, vb).astype(BF)
        dp = dot(dob, vb, NT)
        dsb = (p * (dp - jnp.sum(p * dp, axis=1, keepdims=True))).astype(BF)
        ds_s[g % 2] = dsb
        dk, dv = dot(dsb.T, qh_s[g]), dot(pb.T, dob)
        if g == 0:
            dk_s[...] = dk
            dv_s[...] = dv
        else:
            dk_s[...] += dk
            dv_s[...] += dv

    def query_grad(g):
        dq = unrot(dot(ds_s[g % 2], kcat[:, :HD]) * SCALE)
        if g < 2:
            g1[:, pl.ds(HD + g * HD, HD)] = dq.astype(BF)
        else:
            g2[:, pl.ds((g - 2) * HD, HD)] = dq.astype(BF)
        gt[pl.ds(HD + g * HD, HD), :] = dq.T.astype(BF)

    head(0)
    two.tick("B", 4)
    two.tick("O", 4)
    two.proj(2, 0)
    two.proj(2, 1)
    head(1)
    two.proj(3, 0)
    two.proj(3, 1)
    query_grad(0)
    query_grad(1)
    two.proj(4, 0)
    queries(2)
    queries(3)
    head(2)
    head(3)
    dk = unrot(dk_s[...] * SCALE)
    dv = dv_s[...]
    gsend[...] = jnp.where(first, dv, dk).astype(BF)
    send(gsend, gother, es.at[1], er.at[1], lpeer)
    mine = jnp.where(first, dk, dv)
    g1[:, pl.ds(0, HD)] = mine.astype(BF)
    gt[pl.ds(0, HD), :] = mine.T.astype(BF)
    query_grad(2)
    query_grad(3)
    arrived(gother, es.at[1], er.at[1], lpeer)
    gt[pl.ds(WC, HD), :] = gother[...].astype(F32).T.astype(BF)

    half_rest = (WC - RF) // 2
    ring_rows = {"K": (0, HD), "X": (HD, RF - HD), "O": (RF, WC - RF), "N": (RF, WC - RF)}
    order = {"K": 0, "X": 1, "O": 2, "N": 3}

    def add(dst, src, base, n, step):
        def body(i, carry):
            r = pl.ds(pl.multiple_of(base + i * step, 16), step)
            dst[r, :] = dst[r, :] + src[r, :]
            return carry

        lax.fori_loop(0, n // step, body, 0)

    def zat(o):
        return (z + NZ + o) % NZ

    def products(o):
        zp = zat(o)

        def body(j, carry):
            xcols = xv[:, pl.ds(pl.multiple_of(zp * 1024 + j * WR, WR), WR)]
            cc, hh = j % 2, j // 2
            both = dot(gt[pl.ds(0, HD), :], xcols) + dot(gt[pl.ds(WC, HD), :], xcols)
            pw[zp, cc, hh, pl.ds(0, HD), :] = both.astype(BF)
            pw[zp, cc, hh, pl.ds(HD, QC), :] = dot(gt[pl.ds(HD, QC), :], xcols).astype(BF)
            return carry

        lax.fori_loop(0, 4, body, 0)
        i = o % NZ
        send(pw.at[zp, 1 - c], rc.at[i], pcs.at[i], pcr.at[i], cpeer)

    def core_sum(o):
        zp, i = zat(o), o % NZ
        arrived(rc.at[i], pcs.at[i], pcr.at[i], cpeer)
        add(pw.at[zp, c, 1 - h], rc.at[i, 1 - h], 0, WC, 128)
        part = pw.at[zp, c, 1 - h, pl.ds(0, RF)]
        send(part, rxf.at[i], pxs.at[i], pxr.at[i], xpeer)
        add(pw.at[zp, c, h], rc.at[i, h], 0, WC, 128)

    def x_sum(o):
        zp, i = zat(o), o % NZ
        arrived(rxf.at[i], pxs.at[i], pxr.at[i], xpeer)
        add(pw.at[zp, c, h], rxf.at[i], 0, RF, 128)

    def z_rows(s, p, k):
        base, n = ring_rows[p]
        return (base, n) if s > 0 else (base + k * (n // 2), n // 2)

    def z_arrived(s, p, k):
        base, n = z_rows(s, p, k)
        ring, i = int(p == "O"), order[p]
        arrived(
            rz.at[s, ring, k, pl.ds(base, n)], pzs.at[s, i, k], pzr.at[s, i, k], znb[1 - k]
        )

    def z_step(s, p, k):
        ring, i = int(p == "O"), order[p]
        hh = 1 - h if p == "O" else h
        zp = zat(SGN[k] * (4 - s))
        if s > 0:
            z_arrived(s - 1, p, k)
            base, n = z_rows(s - 1, p, k)
            add(pw.at[zp, c, hh], rz.at[s - 1, ring, k], base, n, 64)
        base, n = z_rows(s, p, k)
        send(
            pw.at[zp, c, hh, pl.ds(base, n)], rz.at[s, ring, k, pl.ds(base, n)],
            pzs.at[s, i, k], pzr.at[s, i, k], znb[k],
        )

    def total(r, ring):
        rows = pl.ds(r, 128)
        return (
            pw[z, c, 1 - h if ring else h, rows, :].astype(F32)
            + rz[3, ring, 0, rows, :].astype(F32)
            + rz[3, ring, 1, rows, :].astype(F32)
        )

    def z_last(p):
        z_arrived(3, p, 0)
        z_arrived(3, p, 1)
        if p == "K":
            kvb[t] = total(0, 0).T.astype(BF)
            for k, peer in enumerate(tpeers):
                send(kvb.at[t], kvb.at[t], ks.at[k], kr.at[t], peer)
        if p == "X":
            for r in range(HD, RF, 128):
                dwq_ref[:, pl.ds(r - HD, 128)] = total(r, 0).T.astype(BF)
        if p == "O":
            for r in range(RF, WC, 128):
                xfs[pl.ds(r - RF, 128), :] = total(r, 1).astype(BF)
            send(xfs, xfr, pfs.at[0], pfr.at[0], xpeer)
        if p == "N":
            arrived(xfr, pfs.at[0], pfr.at[0], xpeer)
            for r in range(RF, WC, 128):
                s = total(r, 0) + xfr[pl.ds(r - RF, 128), :].astype(F32)
                dwq_ref[:, pl.ds(r - HD, 128)] = s.T.astype(BF)

    def dx_products(i):
        for hf in (0, 1):
            wa = wg1[i, 2 * hf:2 * hf + 2].reshape(2 * WR, C1)
            wb = wg2[i, 2 * hf:2 * hf + 2].reshape(2 * WR, WC - C1)
            r = dot(g1[...], wa, NT) + dot(gother[...], wa[:, :HD], NT) + dot(g2[...], wb, NT)
            dxp[i, :, hf] = r.reshape(4, 80, 512).astype(BF)
        for k in (0, 1):
            send(
                dxp.at[i, (y + 2) % 4, k], ry0.at[i, k], y0s.at[i, k], y0r.at[i, k], ynb[k]
            )

    def y_step(i, k):
        arrived(ry0.at[i, k], y0s.at[i, k], y0r.at[i, k], ynb[1 - k])
        yy = (y + 4 + SGN[k]) % 4
        dxp[i, yy, k] = dxp[i, yy, k] + ry0[i, k]
        send(dxp.at[i, yy], ry1.at[i, k], y1s.at[i, k], y1r.at[i, k], ynb[k])

    def y_last(i):
        for k in (0, 1):
            arrived(ry1.at[i, k], y1s.at[i, k], y1r.at[i, k], ynb[1 - k])
        s = dxp[i, y].astype(F32) + ry1[i, 0].astype(F32) + ry1[i, 1].astype(F32)
        a = jnp.concatenate([s[0, :40], s[1, :40]], axis=0)
        b = jnp.concatenate([s[0, 40:], s[1, 40:]], axis=0)
        keep[i] = jnp.where(first, a, b)
        ls[i] = jnp.where(first, b, a).astype(BF)
        send(ls.at[i], rl.at[i], lls.at[i], llr.at[i], lpeer)

    def l_last(i):
        arrived(rl.at[i], lls.at[i], llr.at[i], lpeer)
        s = (keep[i] + rl[i].astype(F32)).astype(BF)
        dx_ref[:, pl.ds(i * 1024, 512)] = s[:40]
        dx_ref[:, pl.ds(i * 1024 + 512, 512)] = s[40:]

    def kv_last():
        for k, peer in enumerate(tpeers):
            tt = (t + 1 + k) % 8
            arrived(kvb.at[tt], ks.at[k], kr.at[tt], peer)
        for yy in range(4):
            for ll in range(2):
                dkv_ref[ll, :, pl.ds(yy * HD, HD)] = kvb[yy * 2 + ll]

    steps = {
        "P": products, "S": core_sum, "A": x_sum, "Z": z_step, "ZL": z_last,
        "D": dx_products, "Y": y_step, "YL": y_last, "LL": l_last, "FIN": kv_last,
    }
    for name, *which in PLAN:
        steps[name](*which)
    for copy in sends:
        copy.wait_send()


def tables():
    i = np.arange(HD // 2, dtype=np.float64)
    ang = np.arange(L, dtype=np.float64)[:, None] * np.exp(i * (-2.0 * math.log(10000.0) / HD))
    cos, sin = np.cos(ang), np.sin(ang)
    return (
        np.concatenate([cos, cos], axis=1).astype(np.float32),
        np.concatenate([-sin, sin], axis=1).astype(np.float32),
    )


def place(a, b, c, d, oa, ob, oc, od, va, vb, vc, vd, sem):
    ways = ((a, va, oa), (b, vb, ob), (c, vc, oc), (d, vd, od))
    into = [pltpu.make_async_copy(src, mid, sem.at[0, i]) for i, (src, mid, _) in enumerate(ways)]
    out = [pltpu.make_async_copy(mid, dst, sem.at[1, i]) for i, (_, mid, dst) in enumerate(ways)]
    for copy in into:
        copy.start()
    for first, second in zip(into, out):
        first.wait()
        second.start()
    for copy in out:
        copy.wait()


def per_device(inputs, query_weight, kv_weight, out_grad):
    cos, sin = tables()
    vm = pl.BlockSpec(memory_space=pltpu.VMEM)
    anywhere = pl.BlockSpec(memory_space=pl.ANY)
    dma = pltpu.SemaphoreType.DMA
    shapes = (
        jax.ShapeDtypeStruct((L, QC), BF),
        jax.ShapeDtypeStruct((WR, QC), BF),
        jax.ShapeDtypeStruct((2, WR, QC), BF),
        jax.ShapeDtypeStruct((40, 8192), BF),
    )
    results = pl.pallas_call(
        kernel,
        out_shape=shapes,
        in_specs=[anywhere] * 6,
        out_specs=(vm, vm, vm, vm),
        scratch_shapes=[
            pltpu.VMEM((L, QC), BF),
            pltpu.VMEM((L, HD), F32),
            pltpu.VMEM((L, HD), F32),
            pltpu.VMEM((L, 8192), BF),
            pltpu.VMEM((NZ, 4, WR, C1), BF),
            pltpu.VMEM((NZ, 4, WR, WC - C1), BF),
            pltpu.VMEM((L, WC), F32),
            pltpu.VMEM((L, HD), F32),
            pltpu.VMEM((L, HD), F32),
            pltpu.VMEM((L, C1), BF),
            pltpu.VMEM((L, WC - C1), BF),
            pltpu.VMEM((L, HD), BF),
            pltpu.VMEM((L, HD), BF),
            pltpu.VMEM((WC + HD, L), BF),
            pltpu.VMEM((HEADS, L, HD), BF),
            pltpu.VMEM((HEADS, L, 2 * HD), BF),
            pltpu.VMEM((L, 2 * HD), BF),
            pltpu.VMEM((L, HD), BF),
            pltpu.VMEM((2, L, L), BF),
            pltpu.VMEM((L, HD), F32),
            pltpu.VMEM((L, HD), F32),
            pltpu.VMEM((NZ, 2, 2, WC, WR), BF),
            pltpu.VMEM((NZ, 2, WC, WR), BF),
            pltpu.VMEM((4, 2, 2, WC, WR), BF),
            pltpu.VMEM((NZ, RF, WR), BF),
            pltpu.VMEM((WC - RF, WR), BF),
            pltpu.VMEM((WC - RF, WR), BF),
            pltpu.VMEM((8, 4, 2, 80, 512), BF),
            pltpu.VMEM((8, 2, 80, 512), BF),
            pltpu.VMEM((8, 2, 2, 80, 512), BF),
            pltpu.VMEM((8, 80, 512), F32),
            pltpu.VMEM((8, 80, 512), BF),
            pltpu.VMEM((8, 80, 512), BF),
            pltpu.VMEM((8, WR, HD), BF),
            dma((7,)),
            dma((2, 3, 2, 5)), dma((2, 3, 2, 5)),
            dma((2, 2, 2, 5)), dma((2, 2, 2, 5)),
            dma((2, 4, 2, 5)), dma((2, 4, 2, 5)),
            dma((2,)), dma((2,)),
            dma((8,)), dma((8,)),
            dma((8,)), dma((8,)),
            dma((4, 4, 2)), dma((4, 4, 2)),
            dma((1,)), dma((1,)),
            dma((8, 2)), dma((8, 2)),
            dma((8, 2)), dma((8, 2)),
            dma((8,)), dma((8,)),
            dma((7,)), dma((8,)),
        ],
        compiler_params=pltpu.CompilerParams(
            collective_id=0, has_side_effects=True, vmem_limit_bytes=60 * 2**20
        ),
        cost_estimate=pl.CostEstimate(
            flops=14_000_000_000, bytes_accessed=8_000_000, transcendentals=410_000
        ),
        name="attention_step",
    )(inputs, query_weight, kv_weight, out_grad, cos, sin)
    return pl.pallas_call(
        place,
        out_shape=shapes,
        in_specs=[anywhere] * 4,
        out_specs=(anywhere,) * 4,
        scratch_shapes=[pltpu.VMEM(s.shape, s.dtype) for s in shapes] + [dma((2, 4))],
        name="place",
    )(*results)


def solution(mesh):
    return jax.shard_map(
        per_device,
        mesh=mesh,
        in_specs=(P("blk", None), P("blk", "tensor"), P(None, "blk", None), P("blk", "tensor")),
        out_specs=(
            P("blk", "tensor"),
            P("blk", "tensor"),
            P(None, "blk", None),
            P(("blk", "tensor"), None),
        ),
        check_vma=False,
    )
```

time: 155 us -> 131 us (0.85)
  Pallas kernels: 145 us -> 130 us
  local copies, waits for them, and re-layouts: 8.24 us -> 0 us
  other arithmetic: 1.7 us -> 0 us
    pallas_call x1 -> x2, Pallas kernels: 145 us -> 130 us  [the longest x1 128 us: per_device(): pl.pallas_call(kernel, out_shape=shapes, in_specs=[anywhere] * 6, out_spe...]
    unnamed x6 -> x0, local copies, waits for them, and re-layouts: 8.23 us -> none
    concatenate x1 -> x0, other arithmetic: 1.7 us -> none  [per_device(): w = jnp.concatenate([query_weight, kv], axis=1)]
where the time goes in v2:
time: 131 us
  Pallas kernels  130 us (99%)
    pallas_call x1, Pallas kernels, per_device(): pl.pallas_call(kernel, out_shape=shapes, in_specs=[anywhere] * 6, out_spe...  128 us

profile of v2, /device:TPU:1, one launch (start us, length us, event | category | flops | bytes accessed | tf_op | source)
XLA Modules:
  0.0 130.8 jit_solution(14206817645322077474)
XLA Ops:
  0.6 127.7 %attention_step.1 = (bf16[320,512]{1,0:T(8,128)(2,1)}, bf16[256,512]{1,0:T(8,128)(2,1)}, bf16[2,256,512]{2,1,0:T(8,128)(2,1)}, bf16[40,8192]{1,0:T(8,128)(2,1)}) custom-call(bf16[320,8192]{1,0:T(8,128)(2,1)} %x_hbm.1, bf16[256,512]{1,0:T(8,128)(2,1)} %wq_hbm.1, bf16[2,256,512]{2,1,0:T(8,128)(2,1)} %kv_hbm.1, bf16[320,512]{1,0:T(8,128)(2,1)} %do_hbm.1, ...), custom_call_target="tpu_custom_call" | custom-call | flops 14000000000 | bytes 8000000 | tf_op jit(solution)/shard_map/attention_step/pallas_call | solution.py:541
  128.4 2.3 %place.1 = (bf16[320,512]{1,0:T(8,128)(2,1)}, bf16[256,512]{1,0:T(8,128)(2,1)}, bf16[2,256,512]{2,1,0:T(8,128)(2,1)}, bf16[40,8192]{1,0:T(8,128)(2,1)}) custom-call(bf16[320,512]{1,0:T(8,128)(2,1)} %get-tuple-element.8.a, bf16[256,512]{1,0:T(8,128)(2,1)} %get-tuple-element.9.b, bf16[2,256,512]{2,1,0:T(8,128)(2,1)} %get-tuple-element.10.c, ...), custom_call_target="tpu_custom_call" | custom-call | tf_op jit(solution)/shard_map/place/pallas_call | solution.py:603

commit v3 on v2

--- a/solution.py
+++ b/solution.py
@@ -18,7 +18,7 @@
 QC = 512
 AF = 160
 C1 = 384
-RF = 256
+DIRECT = 6
 MESH = pl.DeviceIdType.MESH
 BF = jnp.bfloat16
 F32 = jnp.float32
@@ -29,22 +29,28 @@
 
 
 PLAN = (
-    ("P", 4), ("D", 0), ("P", 3), ("D", 1), ("P", -3), ("S", 4), ("Z", 0, "O", 0),
-    ("Z", 0, "O", 1), ("Z", 0, "N", 0), ("Z", 0, "N", 1), ("S", 3), ("Y", 0, 0), ("Y", 0, 1),
-    ("D", 2), ("P", 2), ("S", -3), ("Y", 1, 0), ("Y", 1, 1), ("D", 3), ("Z", 1, "O", 0),
-    ("Z", 1, "O", 1), ("A", 4), ("Z", 0, "K", 0), ("Z", 0, "K", 1), ("Z", 0, "X", 0),
-    ("Z", 0, "X", 1), ("S", 2), ("Z", 1, "N", 0), ("Z", 1, "N", 1), ("YL", 0), ("P", -2),
-    ("A", 3), ("Y", 2, 0), ("Y", 2, 1), ("D", 4), ("P", 1), ("D", 5), ("Z", 2, "O", 0), ("A", -3),
-    ("S", -2), ("Z", 1, "K", 0), ("Z", 1, "K", 1), ("Z", 1, "X", 0), ("Z", 1, "X", 1),
-    ("Z", 2, "O", 1), ("YL", 1), ("A", 2), ("S", 1), ("Y", 3, 0), ("Y", 3, 1), ("LL", 0),
-    ("P", -1), ("D", 6), ("P", 0), ("Z", 2, "N", 0), ("Z", 2, "N", 1), ("A", -2), ("YL", 2),
-    ("Z", 2, "K", 1), ("S", -1), ("Y", 4, 0), ("Y", 4, 1), ("LL", 1), ("D", 7), ("Z", 2, "X", 1),
-    ("A", 1), ("S", 0), ("Z", 3, "O", 0), ("Y", 5, 0), ("Y", 5, 1), ("LL", 2), ("Z", 2, "K", 0),
-    ("Z", 2, "X", 0), ("Z", 3, "O", 1), ("YL", 3), ("A", -1), ("Y", 6, 0), ("Y", 6, 1), ("A", 0),
-    ("Z", 3, "N", 0), ("Z", 3, "N", 1), ("LL", 3), ("YL", 4), ("Z", 3, "K", 1), ("Z", 3, "X", 1),
-    ("Y", 7, 0), ("Y", 7, 1), ("Z", 3, "K", 0), ("LL", 4), ("YL", 5), ("Z", 3, "X", 0),
-    ("ZL", "O"), ("YL", 6), ("LL", 5), ("ZL", "K"), ("YL", 7), ("ZL", "X"), ("ZL", "N"),
-    ("LL", 6), ("LL", 7), ("FIN",),
+    ("P", 1, 4), ("PR", 2), ("T4",), ("PR", 3), ("P", 1, 0), ("P", 1, -3), ("S", 1, 4),
+    ("Z", 0, "N", 1), ("PR", 4), ("H", 2), ("H", 3), ("HS",), ("Z", 0, "O", 0), ("Z", 0, "O", 1),
+    ("P", 1, 1), ("P", 1, 3), ("P", 1, 2), ("Z", 0, "N", 0), ("S", 1, -3), ("QG", 2), ("QG", 3),
+    ("P", 1, -2), ("Z", 1, "N", 1), ("S", 1, 3), ("Z", 1, "O", 0), ("KV",), ("D", 7), ("D", 3),
+    ("P", 2, 4), ("Z", 1, "N", 0), ("D", 4), ("D", 5), ("P", 2, 3), ("S", 2, 4), ("Z", 0, "M", 0),
+    ("Z", 0, "Q", 1), ("Z", 1, "O", 1), ("Y", 3, 1), ("Y", 3, 0), ("Z", 0, "Q", 0), ("P", 2, -3),
+    ("P", 2, -1), ("Z", 0, "M", 1), ("P", 2, 2), ("S", 2, 3), ("Y", 4, 1), ("P", 2, -2),
+    ("Y", 4, 0), ("S", 2, -3), ("Z", 1, "M", 0), ("Z", 1, "Q", 1), ("S", 2, -1), ("D", 2),
+    ("A", 2, 4), ("Z", 0, "K", 0), ("Z", 0, "K", 1), ("Y", 5, 0), ("S", 2, -2), ("Y", 5, 1),
+    ("Z", 1, "Q", 0), ("Z", 1, "M", 1), ("S", 2, 2), ("P", 2, 1), ("D", 6), ("Z", 2, "M", 0),
+    ("Z", 2, "Q", 1), ("D", 1), ("A", 2, 3), ("A", 2, -3), ("Z", 1, "K", 0), ("S", 2, 1),
+    ("Z", 1, "K", 1), ("S", 1, -2), ("Y", 2, 0), ("Y", 2, 1), ("A", 2, -1), ("P", 2, 0),
+    ("Z", 2, "O", 1), ("Z", 2, "Q", 0), ("A", 2, -2), ("D", 0), ("S", 1, 2), ("Z", 2, "M", 1),
+    ("Z", 2, "O", 0), ("YL", 5), ("YL", 4), ("Y", 1, 0), ("Y", 1, 1), ("LQ", 7), ("YL", 3),
+    ("S", 2, 0), ("A", 2, 2), ("Z", 2, "K", 1), ("Z", 2, "K", 0), ("P", 1, -1), ("Z", 3, "Q", 1),
+    ("YL", 2), ("Z", 3, "Q", 0), ("Z", 2, "N", 0), ("LQ", 6), ("S", 1, 0), ("A", 2, 1),
+    ("Y", 0, 0), ("Z", 2, "N", 1), ("Y", 0, 1), ("S", 1, -1), ("Z", 3, "K", 0), ("Z", 3, "K", 1),
+    ("Z", 3, "O", 1), ("YL", 1), ("Z", 3, "M", 1), ("YQ", 7, 1), ("S", 1, 1), ("YQ", 6, 1),
+    ("ZL", "Q"), ("YQ", 6, 0), ("Z", 3, "O", 0), ("Z", 3, "M", 0), ("A", 2, 0), ("YQ", 7, 0),
+    ("YL", 0), ("Z", 3, "N", 1), ("Z", 3, "N", 0), ("ZL", "K"), ("ZL", "O"), ("LL", 1), ("LL", 4),
+    ("LL", 3), ("LL", 0), ("LL", 2), ("FQ", 6), ("ZL", "M"), ("FQ", 7), ("FIN",), ("LL", 5),
+    ("ZL", "N"),
 )
 
 
@@ -57,7 +63,7 @@
     att_ref, dwq_ref, dkv_ref, dx_ref,
     do_ref, cos_ref, sin_ref, xv, wg1, wg2, acc, kvs, kvr, g1, g2, gother, gsend, gt,
     qh_s, qcat, kcat, vb_s, ds_s, dk_s, dv_s, pw, rc, rz, rxf, xfs, xfr,
-    dxp, ry0, ry1, keep, ls, rl, kvb,
+    dxp, ry0, ry1, keep, ls, rl, dxq, rlq, ry0q, ry1q, kvb,
     lsem, zs, zr, xs, xr, cs, cr, es, er,
     pcs, pcr, pxs, pxr, pzs, pzr, pfs, pfr, y0s, y0r, y1s, y1r, lls, llr, ks, kr,
 ):
@@ -328,43 +334,49 @@
             g1[:, pl.ds(HD + g * HD, HD)] = dq.astype(BF)
         else:
             g2[:, pl.ds((g - 2) * HD, HD)] = dq.astype(BF)
-        gt[pl.ds(HD + g * HD, HD), :] = dq.T.astype(BF)
+        gt[pl.ds((g if g < 2 else g + 1) * HD, HD), :] = dq.T.astype(BF)
 
     head(0)
-    two.tick("B", 4)
-    two.tick("O", 4)
-    two.proj(2, 0)
-    two.proj(2, 1)
     head(1)
-    two.proj(3, 0)
-    two.proj(3, 1)
     query_grad(0)
     query_grad(1)
-    two.proj(4, 0)
-    queries(2)
-    queries(3)
-    head(2)
-    head(3)
-    dk = unrot(dk_s[...] * SCALE)
-    dv = dv_s[...]
-    gsend[...] = jnp.where(first, dv, dk).astype(BF)
-    send(gsend, gother, es.at[1], er.at[1], lpeer)
-    mine = jnp.where(first, dk, dv)
-    g1[:, pl.ds(0, HD)] = mine.astype(BF)
-    gt[pl.ds(0, HD), :] = mine.T.astype(BF)
-    query_grad(2)
-    query_grad(3)
-    arrived(gother, es.at[1], er.at[1], lpeer)
-    gt[pl.ds(WC, HD), :] = gother[...].astype(F32).T.astype(BF)
-
-    half_rest = (WC - RF) // 2
-    ring_rows = {"K": (0, HD), "X": (HD, RF - HD), "O": (RF, WC - RF), "N": (RF, WC - RF)}
-    order = {"K": 0, "X": 1, "O": 2, "N": 3}
-
-    def add(dst, src, base, n, step):
+
+    def last_tick():
+        two.tick("B", 4)
+        two.tick("O", 4)
+
+    def projections(d):
+        two.proj(d, 0)
+        if d < 4:
+            two.proj(d, 1)
+        else:
+            queries(2)
+            queries(3)
+
+    def send_kv_grad():
+        dk, dv = unrot(dk_s[...] * SCALE), dv_s[...]
+        gsend[...] = jnp.where(first, dv, dk).astype(BF)
+        send(gsend, gother, es.at[1], er.at[1], lpeer)
+        mine = jnp.where(first, dk, dv)
+        g1[:, pl.ds(0, HD)] = mine.astype(BF)
+        gt[pl.ds(2 * HD, HD), :] = mine.T.astype(BF)
+
+    def kv_grad():
+        arrived(gother, es.at[1], er.at[1], lpeer)
+        gt[pl.ds(WC, HD), :] = gother[...].astype(F32).T.astype(BF)
+
+    pieces = {
+        "N": (0, 0, 2 * HD), "O": (1, 0, 2 * HD),
+        "K": (0, 2 * HD, HD), "M": (0, 3 * HD, 2 * HD), "Q": (1, 3 * HD, 2 * HD),
+    }
+    order = {p: i for i, p in enumerate(pieces)}
+    group_rows = {1: (0, 2 * HD), 2: (2 * HD, 3 * HD)}
+
+    def add(dst, src, base, n, step, shift=0):
         def body(i, carry):
-            r = pl.ds(pl.multiple_of(base + i * step, 16), step)
-            dst[r, :] = dst[r, :] + src[r, :]
+            at = pl.multiple_of(base + i * step, 16)
+            r = pl.ds(at, step)
+            dst[r, :] = dst[r, :] + src[pl.ds(pl.multiple_of(at - shift, 16), step), :]
             return carry
 
         lax.fori_loop(0, n // step, body, 0)
@@ -372,48 +384,60 @@
     def zat(o):
         return (z + NZ + o) % NZ
 
-    def products(o):
+    def products(g, o):
         zp = zat(o)
 
         def body(j, carry):
             xcols = xv[:, pl.ds(pl.multiple_of(zp * 1024 + j * WR, WR), WR)]
             cc, hh = j % 2, j // 2
-            both = dot(gt[pl.ds(0, HD), :], xcols) + dot(gt[pl.ds(WC, HD), :], xcols)
-            pw[zp, cc, hh, pl.ds(0, HD), :] = both.astype(BF)
-            pw[zp, cc, hh, pl.ds(HD, QC), :] = dot(gt[pl.ds(HD, QC), :], xcols).astype(BF)
+            if g == 1:
+                pw[zp, cc, hh, pl.ds(0, 256), :] = dot(gt[pl.ds(0, 256), :], xcols).astype(BF)
+            else:
+                both = dot(gt[pl.ds(256, HD), :], xcols) + dot(gt[pl.ds(WC, HD), :], xcols)
+                pw[zp, cc, hh, pl.ds(256, HD), :] = both.astype(BF)
+                pw[zp, cc, hh, pl.ds(384, 256), :] = dot(
+                    gt[pl.ds(384, 256), :], xcols
+                ).astype(BF)
             return carry
 
         lax.fori_loop(0, 4, body, 0)
         i = o % NZ
-        send(pw.at[zp, 1 - c], rc.at[i], pcs.at[i], pcr.at[i], cpeer)
-
-    def core_sum(o):
+        r = pl.ds(*group_rows[g])
+        at = (g - 1, i)
+        send(pw.at[zp, 1 - c, :, r], rc.at[i, :, r], pcs.at[at], pcr.at[at], cpeer)
+
+    def core_sum(g, o):
         zp, i = zat(o), o % NZ
-        arrived(rc.at[i], pcs.at[i], pcr.at[i], cpeer)
-        add(pw.at[zp, c, 1 - h], rc.at[i, 1 - h], 0, WC, 128)
-        part = pw.at[zp, c, 1 - h, pl.ds(0, RF)]
-        send(part, rxf.at[i], pxs.at[i], pxr.at[i], xpeer)
-        add(pw.at[zp, c, h], rc.at[i, h], 0, WC, 128)
-
-    def x_sum(o):
+        low, n = group_rows[g]
+        r = pl.ds(low, n)
+        at = (g - 1, i)
+        arrived(rc.at[i, :, r], pcs.at[at], pcr.at[at], cpeer)
+        add(pw.at[zp, c, 1 - h], rc.at[i, 1 - h], low, n, 128)
+        if g == 2:
+            part = pw.at[zp, c, 1 - h, pl.ds(low, HD)]
+            send(part, rxf.at[i], pxs.at[i], pxr.at[i], xpeer)
+        add(pw.at[zp, c, h], rc.at[i, h], low, n, 128)
+
+    def x_sum(g, o):
         zp, i = zat(o), o % NZ
         arrived(rxf.at[i], pxs.at[i], pxr.at[i], xpeer)
-        add(pw.at[zp, c, h], rxf.at[i], 0, RF, 128)
+        low = group_rows[g][0]
+        add(pw.at[zp, c, h], rxf.at[i], low, HD, 128, low)
 
     def z_rows(s, p, k):
-        base, n = ring_rows[p]
+        base, n = pieces[p][1:]
         return (base, n) if s > 0 else (base + k * (n // 2), n // 2)
 
     def z_arrived(s, p, k):
         base, n = z_rows(s, p, k)
-        ring, i = int(p == "O"), order[p]
+        ring, i = pieces[p][0], order[p]
         arrived(
             rz.at[s, ring, k, pl.ds(base, n)], pzs.at[s, i, k], pzr.at[s, i, k], znb[1 - k]
         )
 
     def z_step(s, p, k):
-        ring, i = int(p == "O"), order[p]
-        hh = 1 - h if p == "O" else h
+        ring, i = pieces[p][0], order[p]
+        hh = 1 - h if ring else h
         zp = zat(SGN[k] * (4 - s))
         if s > 0:
             z_arrived(s - 1, p, k)
@@ -433,36 +457,82 @@
             + rz[3, ring, 1, rows, :].astype(F32)
         )
 
+    last = {"O": (0, 0), "N": (0, 0), "Q": (1, 2 * HD), "M": (1, 2 * HD)}
+
     def z_last(p):
         z_arrived(3, p, 0)
         z_arrived(3, p, 1)
+        ring, base, n = pieces[p]
         if p == "K":
-            kvb[t] = total(0, 0).T.astype(BF)
+            kvb[t] = total(base, 0).T.astype(BF)
             for k, peer in enumerate(tpeers):
                 send(kvb.at[t], kvb.at[t], ks.at[k], kr.at[t], peer)
-        if p == "X":
-            for r in range(HD, RF, 128):
-                dwq_ref[:, pl.ds(r - HD, 128)] = total(r, 0).T.astype(BF)
-        if p == "O":
-            for r in range(RF, WC, 128):
-                xfs[pl.ds(r - RF, 128), :] = total(r, 1).astype(BF)
-            send(xfs, xfr, pfs.at[0], pfr.at[0], xpeer)
-        if p == "N":
-            arrived(xfr, pfs.at[0], pfr.at[0], xpeer)
-            for r in range(RF, WC, 128):
-                s = total(r, 0) + xfr[pl.ds(r - RF, 128), :].astype(F32)
-                dwq_ref[:, pl.ds(r - HD, 128)] = s.T.astype(BF)
+            return
+        if p in last:
+            i, at = last[p]
+        if p in "OQ":
+            for r in range(0, n, 128):
+                xfs[pl.ds(at + r, 128), :] = total(base + r, 1).astype(BF)
+            rows = pl.ds(at, n)
+            send(xfs.at[rows], xfr.at[rows], pfs.at[i], pfr.at[i], xpeer)
+            return
+        if p in "NM":
+            arrived(xfr.at[pl.ds(at, n)], pfs.at[i], pfr.at[i], xpeer)
+        for r in range(0, n, 128):
+            s = total(base + r, 0)
+            if p in "NM":
+                s = s + xfr[pl.ds(at + r, 128), :].astype(F32)
+            low = base + r if base < 256 else base + r - HD
+            dwq_ref[:, pl.ds(low, 128)] = s.T.astype(BF)
 
     def dx_products(i):
+        halves = []
         for hf in (0, 1):
             wa = wg1[i, 2 * hf:2 * hf + 2].reshape(2 * WR, C1)
             wb = wg2[i, 2 * hf:2 * hf + 2].reshape(2 * WR, WC - C1)
             r = dot(g1[...], wa, NT) + dot(gother[...], wa[:, :HD], NT) + dot(g2[...], wb, NT)
-            dxp[i, :, hf] = r.reshape(4, 80, 512).astype(BF)
+            if i < DIRECT:
+                dxp[i, :, hf] = r.reshape(4, 80, 512).astype(BF)
+            else:
+                halves.append(r.reshape(4, 2, 40, 512))
+        if i < DIRECT:
+            for k in (0, 1):
+                send(
+                    dxp.at[i, (y + 2) % 4, k], ry0.at[i, k], y0s.at[i, k], y0r.at[i, k],
+                    ynb[k],
+                )
+            return
+        j = i - DIRECT
+        for ll in (0, 1):
+            both = jnp.concatenate([halves[0][:, ll], halves[1][:, ll]], axis=1)
+            dxq[j, ll] = both.astype(BF)
+        send(dxq.at[j, 1 - l], rlq.at[j], lls.at[i], llr.at[i], lpeer)
+
+    def lq_step(i):
+        j = i - DIRECT
+        arrived(rlq.at[j], lls.at[i], llr.at[i], lpeer)
+        dxq[j, l] = dxq[j, l] + rlq[j]
         for k in (0, 1):
             send(
-                dxp.at[i, (y + 2) % 4, k], ry0.at[i, k], y0s.at[i, k], y0r.at[i, k], ynb[k]
+                dxq.at[j, l, (y + 2) % 4, :, pl.ds(k * 256, 256)], ry0q.at[j, k],
+                y0s.at[i, k], y0r.at[i, k], ynb[k],
             )
+
+    def yq_step(i, k):
+        j = i - DIRECT
+        arrived(ry0q.at[j, k], y0s.at[i, k], y0r.at[i, k], ynb[1 - k])
+        yy = (y + 4 + SGN[k]) % 4
+        lanes = pl.ds(k * 256, 256)
+        dxq[j, l, yy, :, lanes] = dxq[j, l, yy, :, lanes] + ry0q[j, k]
+        send(dxq.at[j, l, yy], ry1q.at[j, k], y1s.at[i, k], y1r.at[i, k], ynb[k])
+
+    def yq_last(i):
+        j = i - DIRECT
+        for k in (0, 1):
+            arrived(ry1q.at[j, k], y1s.at[i, k], y1r.at[i, k], ynb[1 - k])
+        s = dxq[j, l, y].astype(F32) + ry1q[j, 0].astype(F32) + ry1q[j, 1].astype(F32)
+        dx_ref[:, pl.ds(i * 1024, 512)] = s[:40].astype(BF)
+        dx_ref[:, pl.ds(i * 1024 + 512, 512)] = s[40:].astype(BF)
 
     def y_step(i, k):
         arrived(ry0.at[i, k], y0s.at[i, k], y0r.at[i, k], ynb[1 - k])
@@ -497,6 +567,8 @@
     steps = {
         "P": products, "S": core_sum, "A": x_sum, "Z": z_step, "ZL": z_last,
         "D": dx_products, "Y": y_step, "YL": y_last, "LL": l_last, "FIN": kv_last,
+        "LQ": lq_step, "YQ": yq_step, "FQ": yq_last, "T4": last_tick, "PR": projections,
+        "H": head, "HS": send_kv_grad, "QG": query_grad, "KV": kv_grad,
     }
     for name, *which in PLAN:
         steps[name](*which)
@@ -568,25 +640,29 @@
             pltpu.VMEM((NZ, 2, 2, WC, WR), BF),
             pltpu.VMEM((NZ, 2, WC, WR), BF),
             pltpu.VMEM((4, 2, 2, WC, WR), BF),
-            pltpu.VMEM((NZ, RF, WR), BF),
-            pltpu.VMEM((WC - RF, WR), BF),
-            pltpu.VMEM((WC - RF, WR), BF),
-            pltpu.VMEM((8, 4, 2, 80, 512), BF),
-            pltpu.VMEM((8, 2, 80, 512), BF),
-            pltpu.VMEM((8, 2, 2, 80, 512), BF),
-            pltpu.VMEM((8, 80, 512), F32),
-            pltpu.VMEM((8, 80, 512), BF),
-            pltpu.VMEM((8, 80, 512), BF),
+            pltpu.VMEM((NZ, HD, WR), BF),
+            pltpu.VMEM((4 * HD, WR), BF),
+            pltpu.VMEM((4 * HD, WR), BF),
+            pltpu.VMEM((DIRECT, 4, 2, 80, 512), BF),
+            pltpu.VMEM((DIRECT, 2, 80, 512), BF),
+            pltpu.VMEM((DIRECT, 2, 2, 80, 512), BF),
+            pltpu.VMEM((DIRECT, 80, 512), F32),
+            pltpu.VMEM((DIRECT, 80, 512), BF),
+            pltpu.VMEM((DIRECT, 80, 512), BF),
+            pltpu.VMEM((max(8 - DIRECT, 1), 2, 4, 80, 512), BF),
+            pltpu.VMEM((max(8 - DIRECT, 1), 4, 80, 512), BF),
+            pltpu.VMEM((max(8 - DIRECT, 1), 2, 80, 256), BF),
+            pltpu.VMEM((max(8 - DIRECT, 1), 2, 80, 512), BF),
             pltpu.VMEM((8, WR, HD), BF),
             dma((7,)),
             dma((2, 3, 2, 5)), dma((2, 3, 2, 5)),
             dma((2, 2, 2, 5)), dma((2, 2, 2, 5)),
             dma((2, 4, 2, 5)), dma((2, 4, 2, 5)),
             dma((2,)), dma((2,)),
+            dma((2, 8)), dma((2, 8)),
             dma((8,)), dma((8,)),
-            dma((8,)), dma((8,)),
-            dma((4, 4, 2)), dma((4, 4, 2)),
-            dma((1,)), dma((1,)),
+            dma((4, 5, 2)), dma((4, 5, 2)),
+            dma((2,)), dma((2,)),
             dma((8, 2)), dma((8, 2)),
             dma((8, 2)), dma((8, 2)),
             dma((8,)), dma((8,)),

time: 131 us -> 127 us (0.969)
  Pallas kernels: 130 us -> 126 us
    pallas_call x1, Pallas kernels: 128 us -> 124 us  [per_device(): pl.pallas_call(kernel, out_shape=shapes, in_specs=[anywhere] * 6, out_spe...]
where the time goes in v3:
time: 127 us
  Pallas kernels  126 us (99%)
    pallas_call x1, Pallas kernels, per_device(): pl.pallas_call(kernel, out_shape=shapes, in_specs=[anywhere] * 6, out_spe...  124 us

profile of v3, /device:TPU:1, one launch (start us, length us, event | category | flops | bytes accessed | tf_op | source)
XLA Modules:
  0.0 126.8 jit_solution(7328009762558363414)
XLA Ops:
  0.6 123.6 %attention_step.1 = (bf16[320,512]{1,0:T(8,128)(2,1)}, bf16[256,512]{1,0:T(8,128)(2,1)}, bf16[2,256,512]{2,1,0:T(8,128)(2,1)}, bf16[40,8192]{1,0:T(8,128)(2,1)}) custom-call(bf16[320,8192]{1,0:T(8,128)(2,1)} %x_hbm.1, bf16[256,512]{1,0:T(8,128)(2,1)} %wq_hbm.1, bf16[2,256,512]{2,1,0:T(8,128)(2,1)} %kv_hbm.1, bf16[320,512]{1,0:T(8,128)(2,1)} %do_hbm.1, ...), custom_call_target="tpu_custom_call" | custom-call | flops 14000000000 | bytes 8000000 | tf_op jit(solution)/shard_map/attention_step/pallas_call | solution.py:613
  124.3 2.3 %place.1 = (bf16[320,512]{1,0:T(8,128)(2,1)}, bf16[256,512]{1,0:T(8,128)(2,1)}, bf16[2,256,512]{2,1,0:T(8,128)(2,1)}, bf16[40,8192]{1,0:T(8,128)(2,1)}) custom-call(bf16[320,512]{1,0:T(8,128)(2,1)} %get-tuple-element.8.a, bf16[256,512]{1,0:T(8,128)(2,1)} %get-tuple-element.9.b, bf16[2,256,512]{2,1,0:T(8,128)(2,1)} %get-tuple-element.10.c, ...), custom_call_target="tpu_custom_call" | custom-call | tf_op jit(solution)/shard_map/place/pallas_call | solution.py:679

commit v4 on v3

--- a/solution.py
+++ b/solution.py
@@ -16,7 +16,7 @@
 WR = 256
 WC = 640
 QC = 512
-AF = 160
+AF = 128
 C1 = 384
 DIRECT = 6
 MESH = pl.DeviceIdType.MESH
@@ -29,28 +29,28 @@
 
 
 PLAN = (
-    ("P", 1, 4), ("PR", 2), ("T4",), ("PR", 3), ("P", 1, 0), ("P", 1, -3), ("S", 1, 4),
-    ("Z", 0, "N", 1), ("PR", 4), ("H", 2), ("H", 3), ("HS",), ("Z", 0, "O", 0), ("Z", 0, "O", 1),
-    ("P", 1, 1), ("P", 1, 3), ("P", 1, 2), ("Z", 0, "N", 0), ("S", 1, -3), ("QG", 2), ("QG", 3),
-    ("P", 1, -2), ("Z", 1, "N", 1), ("S", 1, 3), ("Z", 1, "O", 0), ("KV",), ("D", 7), ("D", 3),
-    ("P", 2, 4), ("Z", 1, "N", 0), ("D", 4), ("D", 5), ("P", 2, 3), ("S", 2, 4), ("Z", 0, "M", 0),
-    ("Z", 0, "Q", 1), ("Z", 1, "O", 1), ("Y", 3, 1), ("Y", 3, 0), ("Z", 0, "Q", 0), ("P", 2, -3),
-    ("P", 2, -1), ("Z", 0, "M", 1), ("P", 2, 2), ("S", 2, 3), ("Y", 4, 1), ("P", 2, -2),
-    ("Y", 4, 0), ("S", 2, -3), ("Z", 1, "M", 0), ("Z", 1, "Q", 1), ("S", 2, -1), ("D", 2),
-    ("A", 2, 4), ("Z", 0, "K", 0), ("Z", 0, "K", 1), ("Y", 5, 0), ("S", 2, -2), ("Y", 5, 1),
-    ("Z", 1, "Q", 0), ("Z", 1, "M", 1), ("S", 2, 2), ("P", 2, 1), ("D", 6), ("Z", 2, "M", 0),
-    ("Z", 2, "Q", 1), ("D", 1), ("A", 2, 3), ("A", 2, -3), ("Z", 1, "K", 0), ("S", 2, 1),
-    ("Z", 1, "K", 1), ("S", 1, -2), ("Y", 2, 0), ("Y", 2, 1), ("A", 2, -1), ("P", 2, 0),
-    ("Z", 2, "O", 1), ("Z", 2, "Q", 0), ("A", 2, -2), ("D", 0), ("S", 1, 2), ("Z", 2, "M", 1),
-    ("Z", 2, "O", 0), ("YL", 5), ("YL", 4), ("Y", 1, 0), ("Y", 1, 1), ("LQ", 7), ("YL", 3),
-    ("S", 2, 0), ("A", 2, 2), ("Z", 2, "K", 1), ("Z", 2, "K", 0), ("P", 1, -1), ("Z", 3, "Q", 1),
-    ("YL", 2), ("Z", 3, "Q", 0), ("Z", 2, "N", 0), ("LQ", 6), ("S", 1, 0), ("A", 2, 1),
-    ("Y", 0, 0), ("Z", 2, "N", 1), ("Y", 0, 1), ("S", 1, -1), ("Z", 3, "K", 0), ("Z", 3, "K", 1),
-    ("Z", 3, "O", 1), ("YL", 1), ("Z", 3, "M", 1), ("YQ", 7, 1), ("S", 1, 1), ("YQ", 6, 1),
-    ("ZL", "Q"), ("YQ", 6, 0), ("Z", 3, "O", 0), ("Z", 3, "M", 0), ("A", 2, 0), ("YQ", 7, 0),
-    ("YL", 0), ("Z", 3, "N", 1), ("Z", 3, "N", 0), ("ZL", "K"), ("ZL", "O"), ("LL", 1), ("LL", 4),
-    ("LL", 3), ("LL", 0), ("LL", 2), ("FQ", 6), ("ZL", "M"), ("FQ", 7), ("FIN",), ("LL", 5),
-    ("ZL", "N"),
+    ("P", 1, 4), ("PR", 2), ("T4",), ("PR", 3), ("S", 1, 4), ("Z", 0, "O", 1), ("Z", 0, "N", 1),
+    ("P", 1, -2), ("Z", 0, "O", 0), ("Z", 0, "N", 0), ("PR", 4), ("H", 2), ("H", 3), ("HS",),
+    ("P", 1, 3), ("QG", 3), ("P", 1, -3), ("P", 1, 2), ("S", 1, 3), ("P", 1, 1), ("QG", 2),
+    ("Z", 1, "N", 0), ("S", 1, -3), ("Z", 1, "O", 0), ("Z", 1, "O", 1), ("S", 1, -2),
+    ("Z", 1, "N", 1), ("S", 1, 2), ("KV",), ("D", 6), ("D", 3), ("P", 2, 4), ("D", 4), ("D", 5),
+    ("P", 2, -2), ("S", 2, 4), ("Z", 0, "Q", 1), ("P", 2, -3), ("D", 1), ("Z", 0, "Q", 0),
+    ("Z", 0, "M", 0), ("P", 2, 3), ("Z", 2, "O", 1), ("Z", 0, "M", 1), ("S", 2, -2), ("Y", 3, 1),
+    ("Y", 3, 0), ("S", 2, -3), ("P", 2, -1), ("Y", 4, 1), ("Z", 2, "O", 0), ("P", 1, -1),
+    ("S", 2, 3), ("Z", 1, "Q", 1), ("S", 1, 1), ("Y", 5, 0), ("D", 7), ("Y", 5, 1),
+    ("Z", 1, "Q", 0), ("D", 2), ("P", 2, 2), ("A", 2, 4), ("Z", 0, "K", 0), ("S", 1, -1),
+    ("Z", 1, "M", 0), ("Z", 0, "K", 1), ("P", 2, 0), ("P", 2, 1), ("Z", 1, "M", 1), ("A", 2, -2),
+    ("Y", 1, 1), ("Y", 4, 0), ("A", 2, -3), ("D", 0), ("Z", 3, "O", 0), ("Z", 1, "K", 1),
+    ("A", 2, 3), ("S", 2, 1), ("Y", 1, 0), ("Z", 1, "K", 0), ("Z", 3, "O", 1), ("S", 2, 2),
+    ("S", 2, -1), ("Z", 2, "Q", 0), ("YL", 3), ("P", 1, 0), ("Z", 2, "Q", 1), ("LQ", 7),
+    ("Z", 2, "M", 0), ("LQ", 6), ("S", 1, 0), ("Y", 2, 1), ("Z", 2, "K", 1), ("Y", 2, 0),
+    ("YL", 5), ("S", 2, 0), ("ZL", "O"), ("Z", 2, "M", 1), ("A", 2, 1), ("YL", 4), ("A", 2, 2),
+    ("Z", 2, "K", 0), ("Z", 3, "Q", 1), ("YQ", 7, 0), ("A", 2, -1), ("LL", 3), ("Z", 3, "Q", 0),
+    ("Z", 3, "K", 1), ("YQ", 6, 0), ("YQ", 7, 1), ("Y", 0, 0), ("YL", 1), ("Y", 0, 1),
+    ("Z", 2, "N", 1), ("YQ", 6, 1), ("Z", 3, "K", 0), ("Z", 2, "N", 0), ("Z", 3, "M", 0),
+    ("Z", 3, "M", 1), ("YL", 2), ("ZL", "Q"), ("A", 2, 0), ("ZL", "K"), ("LL", 4), ("FQ", 7),
+    ("Z", 3, "N", 0), ("Z", 3, "N", 1), ("YL", 0), ("FQ", 6), ("LL", 5), ("LL", 2), ("LL", 1),
+    ("ZL", "M"), ("ZL", "N"), ("FIN",), ("LL", 0),
 )
 
 

time: 127 us -> 125 us (0.984)
  Pallas kernels: 126 us -> 124 us
    pallas_call x1, Pallas kernels: 124 us -> 122 us  [per_device(): pl.pallas_call(kernel, out_shape=shapes, in_specs=[anywhere] * 6, out_spe...]
where the time goes in v4:
time: 125 us
  Pallas kernels  124 us (99%)
    pallas_call x1, Pallas kernels, per_device(): pl.pallas_call(kernel, out_shape=shapes, in_specs=[anywhere] * 6, out_spe...  122 us

profile of v4, /device:TPU:1, one launch (start us, length us, event | category | flops | bytes accessed | tf_op | source)
XLA Modules:
  0.0 125.0 jit_solution(4566566480341210889)
XLA Ops:
  0.6 121.8 %attention_step.1 = (bf16[320,512]{1,0:T(8,128)(2,1)}, bf16[256,512]{1,0:T(8,128)(2,1)}, bf16[2,256,512]{2,1,0:T(8,128)(2,1)}, bf16[40,8192]{1,0:T(8,128)(2,1)}) custom-call(bf16[320,8192]{1,0:T(8,128)(2,1)} %x_hbm.1, bf16[256,512]{1,0:T(8,128)(2,1)} %wq_hbm.1, bf16[2,256,512]{2,1,0:T(8,128)(2,1)} %kv_hbm.1, bf16[320,512]{1,0:T(8,128)(2,1)} %do_hbm.1, ...), custom_call_target="tpu_custom_call" | custom-call | flops 14000000000 | bytes 8000000 | tf_op jit(solution)/shard_map/attention_step/pallas_call | solution.py:613
  122.5 2.3 %place.1 = (bf16[320,512]{1,0:T(8,128)(2,1)}, bf16[256,512]{1,0:T(8,128)(2,1)}, bf16[2,256,512]{2,1,0:T(8,128)(2,1)}, bf16[40,8192]{1,0:T(8,128)(2,1)}) custom-call(bf16[320,512]{1,0:T(8,128)(2,1)} %get-tuple-element.8.a, bf16[256,512]{1,0:T(8,128)(2,1)} %get-tuple-element.9.b, bf16[2,256,512]{2,1,0:T(8,128)(2,1)} %get-tuple-element.10.c, ...), custom_call_target="tpu_custom_call" | custom-call | tf_op jit(solution)/shard_map/place/pallas_call | solution.py:679
